TPU v7x, 512 devices: a whole 4x4x16 slice. The times are simulated.
512 devices in a mesh: grp: 16 (over z), seq: 32 (over y, x, core).
Axes of the slice: x: 4, y: 4, z: 16, core: 2. Of those that a mesh axis runs over, the one named last changes fastest.
Arguments:
- row_query: bfloat16 [1024, 128, 768], P(('grp', 'seq')), may hold values from -6 to 6
- row_key: bfloat16 [1024, 128, 768], P(('grp', 'seq')), may hold values from -6 to 6
- row_value: bfloat16 [1024, 128, 768], P(('grp', 'seq')), may hold values from -6 to 6
- column_weight: bfloat16 [768, 2304], P(None, 'grp'), may hold values from -0.21875 to 0.21875
- cotangent: bfloat16 [1024, 128, 768], P('grp', 'seq'), may hold values from -6 to 6
Outputs:
- column_output: bfloat16 [1024, 128, 768], P('grp', 'seq')
- grad_query: bfloat16 [1024, 128, 768], P(('grp', 'seq'))
- grad_key: bfloat16 [1024, 128, 768], P(('grp', 'seq'))
- grad_value: bfloat16 [1024, 128, 768], P(('grp', 'seq'))
All inputs are finite; a program needn't handle non-finite values.
Results may differ from a plain program's by a relative error of at most 0.013.
Values may be sent and summed in bfloat16 or wider, within the bound.
A program may use at most 64 MiB of HBM per device.

v0:
```python
import math

import jax
import jax.numpy as jnp
from jax import lax
from jax.sharding import PartitionSpec as P

HEADS = 12
HEAD_DIM = 64


def softmax_rows(logits):
    shifted = jnp.exp(logits - jnp.max(logits, axis=-1, keepdims=True))
    return shifted / jnp.sum(shifted, axis=-1, keepdims=True)


def column_pass(inputs, packed, incoming):
    f32 = jnp.float32
    rows, cols, width = inputs.shape
    packed = packed.reshape(rows, cols, 3, HEADS, HEAD_DIM)
    query = packed[:, :, 0]
    keys = packed[:, :, 1]
    values = packed[:, :, 2]
    factor = 1.0 / math.sqrt(HEAD_DIM)
    logits = jnp.einsum("ichd,jchd->chij", query, keys, preferred_element_type=f32) * factor
    weights = softmax_rows(logits)
    weights_low = weights.astype(jnp.bfloat16)
    attended = jnp.einsum("chij,jchd->ichd", weights_low, values, preferred_element_type=f32)
    output = (inputs.astype(f32) + attended.reshape(rows, cols, width)).astype(jnp.bfloat16)
    upstream = incoming.reshape(rows, cols, HEADS, HEAD_DIM)
    slope = jnp.einsum("ichd,jchd->chij", upstream, values, preferred_element_type=f32)
    grad_values = jnp.einsum(
        "chij,ichd->jchd", weights_low, upstream, preferred_element_type=f32
    ).astype(jnp.bfloat16)
    grad_logits = (
        weights * (slope - jnp.sum(weights * slope, axis=-1, keepdims=True)) * factor
    ).astype(jnp.bfloat16)
    grad_query = jnp.einsum(
        "chij,jchd->ichd", grad_logits, keys, preferred_element_type=f32
    ).astype(jnp.bfloat16)
    grad_keys = jnp.einsum(
        "chij,ichd->jchd", grad_logits, query, preferred_element_type=f32
    ).astype(jnp.bfloat16)
    packed_grad = jnp.stack([grad_query, grad_keys, grad_values], axis=2).reshape(
        rows * cols, 3 * width
    )
    return (output, packed_grad)


def on_device(row_query, row_key, row_value, column_weight, cotangent):
    f32 = jnp.float32
    own_rows, columns, width = row_query.shape
    depth_rows = own_rows * lax.axis_size("seq")
    scale = 1.0 / (math.sqrt(HEAD_DIM) * math.sqrt(depth_rows))
    query = row_query.reshape(own_rows, columns, HEADS, HEAD_DIM)
    keys = row_key.reshape(own_rows, columns, HEADS, HEAD_DIM)
    values = row_value.reshape(own_rows, columns, HEADS, HEAD_DIM)
    local_scores = jnp.einsum("rihd,rjhd->hij", query, keys, preferred_element_type=f32)
    probs = softmax_rows(lax.psum(local_scores, "seq") * scale)
    probs_low = probs.astype(jnp.bfloat16)
    hidden = jnp.einsum("hij,rjhd->rihd", probs_low, values, preferred_element_type=f32)
    hidden = hidden.astype(jnp.bfloat16).reshape(own_rows, columns, width)
    column_inputs = lax.all_to_all(hidden, "seq", split_axis=1, concat_axis=0, tiled=True)
    block_rows, own_columns, _ = column_inputs.shape
    flat_inputs = column_inputs.reshape(block_rows * own_columns, width)
    full_weight = lax.all_gather(column_weight, "grp", axis=1, tiled=True)
    packed = jnp.dot(flat_inputs, full_weight, preferred_element_type=f32).astype(jnp.bfloat16)
    column_output, packed_grad = column_pass(column_inputs, packed, cotangent)
    incoming_flat = cotangent.reshape(block_rows * own_columns, width).astype(f32)
    back = incoming_flat + lax.dot_general(
        packed_grad, full_weight, (((1,), (1,)), ((), ())), preferred_element_type=f32
    )
    back = back.astype(jnp.bfloat16).reshape(block_rows, own_columns, width)
    upstream = lax.all_to_all(back, "seq", split_axis=0, concat_axis=1, tiled=True).reshape(
        own_rows, columns, HEADS, HEAD_DIM
    )
    grad_value = jnp.einsum(
        "hij,rihd->rjhd", probs_low, upstream, preferred_element_type=f32
    ).astype(jnp.bfloat16)
    local_slope = jnp.einsum("rihd,rjhd->hij", upstream, values, preferred_element_type=f32)
    slope = lax.psum(local_slope, "seq")
    grad_scores = (probs * (slope - jnp.sum(probs * slope, axis=-1, keepdims=True)) * scale).astype(
        jnp.bfloat16
    )
    grad_query = jnp.einsum("hij,rjhd->rihd", grad_scores, keys, preferred_element_type=f32).astype(
        jnp.bfloat16
    )
    grad_key = jnp.einsum("hij,rihd->rjhd", grad_scores, query, preferred_element_type=f32).astype(
        jnp.bfloat16
    )
    return (
        column_output,
        grad_query.reshape(own_rows, columns, width),
        grad_key.reshape(own_rows, columns, width),
        grad_value.reshape(own_rows, columns, width),
    )


def solution(mesh):
    in_specs = (
        P(("grp", "seq"), None, None),
        P(("grp", "seq"), None, None),
        P(("grp", "seq"), None, None),
        P(None, "grp"),
        P("grp", "seq", None),
    )
    out_specs = (
        P("grp", "seq", None),
        P(("grp", "seq"), None, None),
        P(("grp", "seq"), None, None),
        P(("grp", "seq"), None, None),
    )
    return jax.shard_map(
        on_device, mesh=mesh, in_specs=in_specs, out_specs=out_specs, check_vma=False
    )
```

profile of v0, /device:TPU:1, one launch (start us, length us, event | category | flops | bytes accessed | tf_op | source)
XLA Modules:
  0.0 399.0 jit_solution(13555306033450018599)
XLA Ops:
  8.0 1.2 copy.132
  9.3 1.4 copy.133
  10.7 1.2 convolution_bitcast_fusion.1
  12.8 139.7 %all-reduce.3.cloned.1.call-done = f32[12,128,128]{2,1,0:T(8,128)} async-done(((f32[12,128,128]{2,1,0:T(8,128)}), f32[12,128,128]{2,1,0:T(8,128)}) %all-reduce.3.cloned.1.call-update) | async-done | bytes 786448 | tf_op jit(solution)/shard_map/psum | solution.py:59
  152.5 2.3 fusion.66
  154.8 4.0 fusion.42
  158.9 1.1 copy.137
  160.0 5.8 %all-to-all-start = ((bf16[2,128,768]{2,0,1:T(2,128)(2,1)}), bf16[2,128,768]{2,0,1:T(2,128)(2,1)S(1)}, u32[]{:S(2)}, u32[]{:S(2)}) async-start(bf16[2,128,768]{2,0,1:T(2,128)(2,1)} %copy.137), calls=%async_computation | async-start | bytes 786432 | tf_op jit(solution)/shard_map/all_to_all | solution.py:63
  165.8 1.6 reshape.88
  168.3 7.6 %all-to-all-done = bf16[2,128,768]{2,0,1:T(2,128)(2,1)S(1)} async-done(((bf16[2,128,768]{2,0,1:T(2,128)(2,1)}), bf16[2,128,768]{2,0,1:T(2,128)(2,1)S(1)}, u32[]{:S(2)}, u32[]{:S(2)}) %all-to-all-start) | async-done | bytes 393248 | tf_op jit(solution)/shard_map/all_to_all | solution.py:63
  177.4 4.1 %convolution_convert_fusion = bf16[256,2304]{1,0:T(8,128)(2,1)} fusion(bf16[256,768]{1,0:T(8,128)(2,1)S(1)} %reshape.67, bf16[768,2304]{0,1:T(8,128)(2,1)} %all-gather.2.cloned.1.call-done), kind=kOutput, calls=%fused_computation.4 | convolution fusion | flops 906559488 | bytes 5111808 | tf_op jit(solution)/shard_map/dot_general | solution.py:67
  181.5 3.4 reshape.68
  185.0 2.1 fusion.65
  187.1 2.1 copy.179
  189.2 4.2 %fusion.67 = (f32[4,12,64]{2,1,0:T(8,128)S(1)}, f32[4,12,64,64]{2,3,1,0:T(8,128)}) fusion(bf16[64,4,1,12,64]{4,3,2,1,0:T(8,128)(2,1)S(1)} %copy-done.9, bf16[64,4,1,12,64]{4,3,2,1,0:T(8,128)(2,1)} %get-tuple-element.20), kind=kOutput, calls=%fused_computation.80 | convolution fusion | flops 25755712 | bytes 1585152 | tf_op jit(solution)/shard_map/sub | solution.py:13
  193.4 2.0 fusion.26
  195.3 4.2 %fusion.10 = bf16[64,4,1,12,64]{0,4,3,1,2:T(8,128)(2,1)S(1)} fusion(f32[4,12,64,64]{3,2,1,0:T(8,128)} %fusion.26, bf16[64,4,1,12,64]{4,3,2,1,0:T(8,128)(2,1)} %get-tuple-element.20, f32[4,12,64,64]{2,3,1,0:T(8,128)} %get-tuple-element.28, f32[4,12,64]{2,1,0:T(8,128)S(1)} %get-tuple-element.27), kind=kOutput, calls=%fused_computation.18 | convolution fusion | flops 26741824 | bytes 2371584 | tf_op jit(solution)/shard_map/chij,jchd->ichd/dot_general | solution.py:38
  199.6 4.9 %fusion.11 = bf16[64,4,1,12,64]{0,4,3,1,2:T(8,128)(2,1)} fusion(f32[4,12,64,64]{3,2,1,0:T(8,128)} %fusion.26, bf16[64,4,1,12,64]{4,3,2,1,0:T(8,128)(2,1)S(1)} %copy-done.9, f32[4,12,64,64]{2,3,1,0:T(8,128)} %get-tuple-element.28, f32[4,12,64]{2,1,0:T(8,128)S(1)} %get-tuple-element.27), kind=kOutput, calls=%fused_computation.19 | convolution fusion | flops 26741824 | bytes 2371584 | tf_op jit(solution)/shard_map/chij,ichd->jchd/dot_general | solution.py:41
  204.5 2.2 fusion.12
  206.8 2.0 pad_maximum_fusion
  208.8 4.1 %copy.155 = bf16[64,4,3,12,64]{4,3,2,1,0:T(8,128)(2,1)S(1)} copy(bf16[64,4,3,12,64]{0,4,3,1,2:T(8,128)(2,1)} %pad_maximum_fusion) | data formatting | bytes 2359296 | tf_op jit(solution)/shard_map/stack | solution.py:44
  212.9 2.8 reshape.71
  215.7 3.6 fusion.17
  220.2 3.9 all-to-all-start.1
  226.6 1.5 fusion.28
  228.1 1.9 copy.145
  230.0 4.5 %all-to-all-done.1 = bf16[64,4,768]{2,1,0:T(4,128)(2,1)S(1)} async-done(((bf16[64,4,768]{2,1,0:T(4,128)(2,1)}), bf16[64,4,768]{2,1,0:T(4,128)(2,1)S(1)}, u32[]{:S(2)}, u32[]{:S(2)}) %all-to-all-start.1) | async-done | bytes 393248 | tf_op jit(solution)/shard_map/all_to_all | solution.py:74
  235.9 1.2 convolution_bitcast_fusion
  238.1 3.9 fusion.19
  243.1 126.3 %all-reduce.5.cloned.1.call-done = f32[12,128,128]{2,1,0:T(8,128)} async-done(((f32[12,128,128]{2,1,0:T(8,128)}), f32[12,128,128]{2,1,0:T(8,128)}) %all-reduce.5.cloned.1.call-update) | async-done | bytes 786448 | tf_op jit(solution)/shard_map/psum | solution.py:81
  369.3 10.1 %fusion.20 = f32[12,128,128]{1,2,0:S(1)} fusion(bf16[12,128,128]{1,2,0:T(8,128)(2,1)S(1)} %bitcast.137, f32[12,128,128]{2,1,0:T(8,128)} %all-reduce.5.cloned.1.call-done, f32[12,128,128]{2,1,0:T(8,128)} %get-tuple-element.26, f32[12,128]{1,0:T(8,128)S(1)} %get-tuple-element.25), kind=kOutput, calls=%fused_computation.32 | convolution fusion | flops 51709568 | bytes 2758656
  380.5 10.0 %fusion.21 = f32[12,128,128]{1,2,0:S(1)} fusion(bf16[12,128,128]{1,2,0:T(8,128)(2,1)S(1)} %bitcast.136, f32[12,128,128]{2,1,0:T(8,128)} %all-reduce.5.cloned.1.call-done, f32[12,128,128]{2,1,0:T(8,128)} %get-tuple-element.26, f32[12,128]{1,0:T(8,128)S(1)} %get-tuple-element.25), kind=kOutput, calls=%fused_computation.33 | convolution fusion | flops 51709568 | bytes 2758656
  (65 shorter events, 12.1 us)
Async XLA Ops:
  8.0 144.5 %all-reduce.3.cloned.1.call-start = ((), (), s32[]{:S(2)}) async-start(), calls=%async_computation.2 | async-start | bytes 1572864 | tf_op jit(solution)/shard_map/psum | solution.py:59
  9.3 2.6 copy-start.2
  9.3 3.2 copy-start.11
  10.7 2.1 copy-start
  11.9 165.5 %all-gather.2.cloned.1.call-start = ((), (), s32[]{:S(2)}) async-start(), calls=%async_computation.3 | async-start | bytes 3760128 | tf_op jit(solution)/shard_map/all_gather | solution.py:66
  158.8 7.0 %copy-start.8 = (bf16[64,4,768]{2,1,0:T(4,128)(2,1)S(1)}, bf16[64,4,768]{2,1,0:T(4,128)(2,1)}, u32[]{:S(2)}) copy-start(bf16[64,4,768]{2,1,0:T(4,128)(2,1)} %param.9) | copy-start | bytes 1179652
  160.0 16.0 %all-to-all-start = ((bf16[2,128,768]{2,0,1:T(2,128)(2,1)}), bf16[2,128,768]{2,0,1:T(2,128)(2,1)S(1)}, u32[]{:S(2)}, u32[]{:S(2)}) async-start(bf16[2,128,768]{2,0,1:T(2,128)(2,1)} %copy.137), calls=%async_computation | async-start | bytes 786432 | tf_op jit(solution)/shard_map/all_to_all | solution.py:63
  187.1 2.1 copy-start.9
  189.2 4.2 %copy-start.6 = (bf16[64,4,1,12,64]{0,4,3,1,2:T(8,128)(2,1)}, bf16[64,4,1,12,64]{0,4,3,1,2:T(8,128)(2,1)S(1)}, u32[]{:S(2)}) copy-start(bf16[64,4,1,12,64]{0,4,3,1,2:T(8,128)(2,1)S(1)} %copy.179) | copy-start | bytes 1179652
  189.2 4.2 %copy-start.4 = (bf16[64,4,12,64]{3,2,1,0:T(8,128)(2,1)S(1)}, bf16[64,4,12,64]{3,2,1,0:T(8,128)(2,1)}, u32[]{:S(2)}) copy-start(bf16[64,4,12,64]{3,2,1,0:T(8,128)(2,1)} %reshape.88) | copy-start | bytes 1179652
  193.4 11.1 %copy-start.15 = (f32[4,12,64]{2,1,0:T(8,128)}, f32[4,12,64]{2,1,0:T(8,128)S(1)}, u32[]{:S(2)}) copy-start(f32[4,12,64]{2,1,0:T(8,128)S(1)} %get-tuple-element.27) | copy-start | bytes 36868
  204.5 2.3 copy-start.10
  219.4 5.1 %copy-start.3 = (bf16[2,128,768]{1,2,0:T(8,128)(2,1)S(1)}, bf16[2,128,768]{1,2,0:T(8,128)(2,1)}, u32[]{:S(2)}) copy-start(bf16[2,128,768]{1,2,0:T(8,128)(2,1)} %copy-done.2) | copy-start | bytes 1179652
  219.4 5.9 %copy-start.1 = (bf16[2,128,768]{1,2,0:T(8,128)(2,1)S(1)}, bf16[2,128,768]{1,2,0:T(8,128)(2,1)}, u32[]{:S(2)}) copy-start(bf16[2,128,768]{1,2,0:T(8,128)(2,1)} %copy-done) | copy-start | bytes 1179652
  219.4 6.6 %copy-start.5 = (f32[32,2,4,768]{3,0,2,1:T(8,128)S(1)}, f32[32,2,4,768]{3,0,2,1:T(8,128)}, u32[]{:S(2)}) copy-start(f32[32,2,4,768]{3,0,2,1:T(8,128)} %get-tuple-element.23) | copy-start | bytes 2359300
  220.2 14.2 %all-to-all-start.1 = ((bf16[64,4,768]{2,1,0:T(4,128)(2,1)}), bf16[64,4,768]{2,1,0:T(4,128)(2,1)S(1)}, u32[]{:S(2)}, u32[]{:S(2)}) async-start(bf16[64,4,768]{2,1,0:T(4,128)(2,1)} %reshape.72), calls=%async_computation.1 | async-start | bytes 786432 | tf_op jit(solution)/shard_map/all_to_all | solution.py:74
  224.1 2.4 copy-start.7
  224.2 2.4 copy-start.16
  224.2 145.2 %all-reduce.5.cloned.1.call-start = ((), (), s32[]{:S(2)}) async-start(), calls=%async_computation.4 | async-start | bytes 1572864 | tf_op jit(solution)/shard_map/psum | solution.py:81
  224.5 2.1 copy-start.14
  242.1 127.3 %copy-start.13 = (bf16[2,128,12,64]{1,3,0,2:T(8,128)(2,1)S(1)}, bf16[2,128,12,64]{1,3,0,2:T(8,128)(2,1)}, u32[]{:S(2)}) copy-start(bf16[2,128,12,64]{1,3,0,2:T(8,128)(2,1)} %copy.161) | copy-start | bytes 1179652
  379.4 1.1 copy-start.12
Sparse Core Ops, SparseCore 0:
  12.1 140.3 all-reduce.2
  237.3 132.0 all-reduce.4
Sparse Core Ops, SparseCore 1:
  14.5 73.8 all-gather.1
where the time goes:
time: 400 us; the launch traced here: 399 us
  waiting for transfers between devices  279 us (70%)
  matrix products  57.3 us (14%)
  local copies, waits for them, and re-layouts  30.5 us (8%)
  between operations  15.9 us (4%)
  starting transfers between devices  10.1 us (3%)
  other arithmetic  6.57 us (2%)
    psum x1, waiting for transfers between devices, on_device(): probs = softmax_rows(lax.psum(local_scores, 'seq') * scale)  140 us
    psum x1, waiting for transfers between devices, on_device(): slope = lax.psum(local_slope, 'seq')  126 us
    unnamed x3, matrix products  24.1 us
  transfers between devices with their start and end apart: 5, of which 4 were waited for; matrix products, arithmetic and copies ran while one was open for 6% of the time, Pallas kernels for 0%

commit v1 on v0

--- a/solution.py
+++ b/solution.py
@@ -47,6 +47,14 @@
     return (output, packed_grad)
 
 
+def scatter_sum(terms):
+    heads, rows, cols = terms.shape
+    members = lax.axis_size("seq")
+    blocks = terms.reshape(heads, members, rows // members, cols).transpose(1, 0, 2, 3)
+    received = lax.all_to_all(blocks, "seq", split_axis=0, concat_axis=0, tiled=True)
+    return jnp.sum(received, axis=0)
+
+
 def on_device(row_query, row_key, row_value, column_weight, cotangent):
     f32 = jnp.float32
     own_rows, columns, width = row_query.shape
@@ -56,8 +64,8 @@
     keys = row_key.reshape(own_rows, columns, HEADS, HEAD_DIM)
     values = row_value.reshape(own_rows, columns, HEADS, HEAD_DIM)
     local_scores = jnp.einsum("rihd,rjhd->hij", query, keys, preferred_element_type=f32)
-    probs = softmax_rows(lax.psum(local_scores, "seq") * scale)
-    probs_low = probs.astype(jnp.bfloat16)
+    probs = softmax_rows(scatter_sum(local_scores) * scale)
+    probs_low = lax.all_gather(probs.astype(jnp.bfloat16), "seq", axis=1, tiled=True)
     hidden = jnp.einsum("hij,rjhd->rihd", probs_low, values, preferred_element_type=f32)
     hidden = hidden.astype(jnp.bfloat16).reshape(own_rows, columns, width)
     column_inputs = lax.all_to_all(hidden, "seq", split_axis=1, concat_axis=0, tiled=True)
@@ -78,10 +86,11 @@
         "hij,rihd->rjhd", probs_low, upstream, preferred_element_type=f32
     ).astype(jnp.bfloat16)
     local_slope = jnp.einsum("rihd,rjhd->hij", upstream, values, preferred_element_type=f32)
-    slope = lax.psum(local_slope, "seq")
+    slope = scatter_sum(local_slope)
     grad_scores = (probs * (slope - jnp.sum(probs * slope, axis=-1, keepdims=True)) * scale).astype(
         jnp.bfloat16
     )
+    grad_scores = lax.all_gather(grad_scores, "seq", axis=1, tiled=True)
     grad_query = jnp.einsum("hij,rjhd->rihd", grad_scores, keys, preferred_element_type=f32).astype(
         jnp.bfloat16
     )

time: 400 us -> 208 us (0.52)
  waiting for transfers between devices: 279 us -> 43.9 us
  blocking collectives: 0 us -> 45.8 us
  matrix products: 57.3 us -> 30.2 us
  starting transfers between devices: 10.1 us -> 35.5 us
    psum x2 -> x0, waiting for transfers between devices: 266 us -> none  [the longest x1 140 us: on_device(): probs = softmax_rows(lax.psum(local_scores, 'seq') * scale)]
    all_gather x0 -> x2, blocking collectives: none -> 45.8 us  [the longest x1 22.9 us: on_device(): grad_scores = lax.all_gather(grad_scores, 'seq', axis=1, tiled=True)]
    unnamed x3, matrix products: 24.1 us -> 1.04 us
    all_to_all x0 -> x2, waiting for transfers between devices: none -> 21.3 us  [scatter_sum(): lax.all_to_all(blocks, 'seq', split_axis=0, concat_axis=0, tiled=True)]
    all_to_all x0 -> x2, starting transfers between devices: none -> 14.4 us  [scatter_sum(): lax.all_to_all(blocks, 'seq', split_axis=0, concat_axis=0, tiled=True)]
    all_to_all x1, starting transfers between devices: 3.89 us -> 16.1 us  [on_device(): lax.all_to_all(back, 'seq', split_axis=0, concat_axis=1, tiled=True)]
    all_gather x1, waiting for transfers between devices: 0.03 us -> 5.51 us  [on_device(): full_weight = lax.all_gather(column_weight, 'grp', axis=1, tiled=True)]
    all_to_all x1, waiting for transfers between devices: 4.46 us -> 8.82 us  [on_device(): lax.all_to_all(back, 'seq', split_axis=0, concat_axis=1, tiled=True)]
  transfers between devices with their start and end apart: 5 -> 5, of which waited for: 4 -> 5; matrix products, arithmetic and copies ran while one was open for 6% -> 9% of each run, Pallas kernels for 0% -> 0%
where the time goes in v1:
time: 208 us; the launch traced here: 207 us
  blocking collectives  45.8 us (22%)
  waiting for transfers between devices  43.9 us (21%)
  starting transfers between devices  35.5 us (17%)
  local copies, waits for them, and re-layouts  32.1 us (15%)
  matrix products  30.2 us (15%)
  between operations  14.5 us (7%)
  other arithmetic  5.17 us (2%)
    all_gather x1, blocking collectives, on_device(): grad_scores = lax.all_gather(grad_scores, 'seq', axis=1, tiled=True)  22.9 us
    all_gather x1, blocking collectives, on_device(): lax.all_gather(probs.astype(jnp.bfloat16), 'seq', axis=1, tiled=True)  22.9 us
    all_to_all x2, waiting for transfers between devices, scatter_sum(): lax.all_to_all(blocks, 'seq', split_axis=0, concat_axis=0, tiled=True)  21.3 us
    all_to_all x1, starting transfers between devices, on_device(): lax.all_to_all(back, 'seq', split_axis=0, concat_axis=1, tiled=True)  16.1 us
    all_to_all x2, starting transfers between devices, scatter_sum(): lax.all_to_all(blocks, 'seq', split_axis=0, concat_axis=0, tiled=True)  14.4 us
    all_to_all x1, waiting for transfers between devices, on_device(): lax.all_to_all(back, 'seq', split_axis=0, concat_axis=1, tiled=True)  8.82 us
    unnamed x45, local copies, waits for them, and re-layouts  8.06 us
    all_to_all x1, waiting for transfers between devices, on_device(): lax.all_to_all(hidden, 'seq', split_axis=1, concat_axis=0, tiled=True)  7.63 us
  transfers between devices with their start and end apart: 5, of which 5 were waited for; matrix products, arithmetic and copies ran while one was open for 9% of the time, Pallas kernels for 0%

profile of v1, /device:TPU:1, one launch (start us, length us, event | category | flops | bytes accessed | tf_op | source)
XLA Modules:
  0.0 207.2 jit_solution(17286295161119283676)
XLA Ops:
  7.9 1.2 copy.181
  9.1 1.4 copy.182
  11.9 10.4 %all-to-all-start = ((f32[32,12,4,128]{3,2,1,0:T(4,128)}), f32[32,12,4,128]{3,2,1,0:T(4,128)S(1)}, u32[]{:S(2)}, u32[]{:S(2)}) async-start(f32[32,12,4,128]{3,2,1,0:T(4,128)} %bitcast.123), calls=%async_computation | async-start | bytes 1572864 | tf_op jit(solution)/shard_map/all_to_all | solution.py:54
  22.6 14.1 %all-to-all-done = f32[32,12,4,128]{3,2,1,0:T(4,128)S(1)} async-done(((f32[32,12,4,128]{3,2,1,0:T(4,128)}), f32[32,12,4,128]{3,2,1,0:T(4,128)S(1)}, u32[]{:S(2)}, u32[]{:S(2)}) %all-to-all-start) | async-done | bytes 786464 | tf_op jit(solution)/shard_map/all_to_all | solution.py:54
  37.1 22.9 %all_gather.9 = bf16[12,128,128]{2,0,1:T(8,128)(2,1)S(1)} all-gather(bf16[12,4,128]{2,0,1:T(8,128)(2,1)S(1)} %copy.184), channel_id=1, replica_groups=mesh['grp'=16,'seq'=32] {'seq'}, dimensions={1}, use_global_device_ids=true | all-gather | bytes 405504 | tf_op jit(solution)/shard_map/all_gather | solution.py:68
  60.8 1.1 copy.189
  61.8 5.0 %all-to-all-start.1 = ((bf16[2,128,768]{2,0,1:T(2,128)(2,1)}), bf16[2,128,768]{2,0,1:T(2,128)(2,1)S(1)}, u32[]{:S(2)}, u32[]{:S(2)}) async-start(bf16[2,128,768]{2,0,1:T(2,128)(2,1)} %copy.189), calls=%async_computation.1 | async-start | bytes 786432 | tf_op jit(solution)/shard_map/all_to_all | solution.py:71
  66.8 1.6 reshape.96
  69.4 7.6 %all-to-all-done.1 = bf16[2,128,768]{2,0,1:T(2,128)(2,1)S(1)} async-done(((bf16[2,128,768]{2,0,1:T(2,128)(2,1)}), bf16[2,128,768]{2,0,1:T(2,128)(2,1)S(1)}, u32[]{:S(2)}, u32[]{:S(2)}) %all-to-all-start.1) | async-done | bytes 393248 | tf_op jit(solution)/shard_map/all_to_all | solution.py:71
  77.0 1.1 fusion.48
  78.5 5.5 %all-gather.2.cloned.1.call-done = bf16[768,2304]{0,1:T(8,128)(2,1)} async-done(((bf16[768,144]{0,1:T(8,128)(2,1)}), bf16[768,2304]{0,1:T(8,128)(2,1)}) %all-gather.2.cloned.1.call-update) | async-done | bytes 3538960 | tf_op jit(solution)/shard_map/all_gather | solution.py:74
  84.0 4.2 %convolution_convert_fusion = bf16[256,2304]{1,0:T(8,128)(2,1)} fusion(bf16[256,768]{1,0:T(8,128)(2,1)S(1)} %reshape.74, bf16[768,2304]{0,1:T(8,128)(2,1)} %all-gather.2.cloned.1.call-done), kind=kOutput, calls=%fused_computation.4 | convolution fusion | flops 906559488 | bytes 5111808 | tf_op jit(solution)/shard_map/dot_general | solution.py:75
  88.1 3.4 %reshape.75 = bf16[64,4,3,12,64]{4,3,2,1,0:T(8,128)(2,1)S(1)} reshape(bf16[256,2304]{1,0:T(8,128)(2,1)} %convolution_convert_fusion) | data formatting | bytes 2359296 | tf_op jit(solution)/shard_map/reshape | solution.py:20
  91.6 2.1 %fusion.51 = (bf16[64,4,1,12,64]{4,3,2,1,0:T(8,128)(2,1)}, bf16[64,4,1,12,64]{4,3,2,1,0:T(8,128)(2,1)}, bf16[64,4,1,12,64]{4,3,2,1,0:T(8,128)(2,1)}) fusion(bf16[64,4,3,12,64]{4,3,2,1,0:T(8,128)(2,1)S(1)} %reshape.75), kind=kLoop, calls=%fused_computation.74 | loop fusion | bytes 2359296 | tf_op jit(solution)/shard_map/slice | solution.py:22
  93.7 2.1 %copy.238 = bf16[64,4,1,12,64]{0,4,3,1,2:T(8,128)(2,1)S(1)} copy(bf16[64,4,1,12,64]{4,3,2,1,0:T(8,128)(2,1)} %get-tuple-element.25) | data formatting | bytes 786432
  95.8 4.2 %fusion.53 = (f32[4,12,64]{2,1,0:T(8,128)S(1)}, f32[4,12,64,64]{2,3,1,0:T(8,128)}) fusion(bf16[64,4,1,12,64]{4,3,2,1,0:T(8,128)(2,1)S(1)} %copy-done.12, bf16[64,4,1,12,64]{4,3,2,1,0:T(8,128)(2,1)} %get-tuple-element.24), kind=kOutput, calls=%fused_computation.76 | convolution fusion | flops 25755712 | bytes 1585152 | tf_op jit(solution)/shard_map/sub | solution.py:13
  100.0 2.0 fusion.20
  102.0 4.2 %fusion.9 = bf16[64,4,1,12,64]{0,4,3,1,2:T(8,128)(2,1)S(1)} fusion(f32[4,12,64,64]{3,2,1,0:T(8,128)} %fusion.20, bf16[64,4,1,12,64]{4,3,2,1,0:T(8,128)(2,1)} %get-tuple-element.24, f32[4,12,64,64]{2,3,1,0:T(8,128)} %get-tuple-element.32, f32[4,12,64]{2,1,0:T(8,128)S(1)} %get-tuple-element.31), kind=kOutput, calls=%fused_computation.17 | convolution fusion | flops 26741824 | bytes 2371584 | tf_op jit(solution)/shard_map/chij,jchd->ichd/dot_general | solution.py:38
  106.2 5.0 %fusion.10 = bf16[64,4,1,12,64]{0,4,3,1,2:T(8,128)(2,1)} fusion(f32[4,12,64,64]{3,2,1,0:T(8,128)} %fusion.20, bf16[64,4,1,12,64]{4,3,2,1,0:T(8,128)(2,1)S(1)} %copy-done.12, f32[4,12,64,64]{2,3,1,0:T(8,128)} %get-tuple-element.32, f32[4,12,64]{2,1,0:T(8,128)S(1)} %get-tuple-element.31), kind=kOutput, calls=%fused_computation.18 | convolution fusion | flops 26741824 | bytes 2371584 | tf_op jit(solution)/shard_map/chij,ichd->jchd/dot_general | solution.py:41
  111.1 2.2 %fusion.11 = bf16[64,4,1,12,64]{0,4,3,1,2:T(8,128)(2,1)S(1)} fusion(bf16[64,4,12,64]{3,2,1,0:T(8,128)(2,1)S(1)} %copy-done.6, f32[4,12,64,64]{2,3,1,0:T(8,128)} %get-tuple-element.32, f32[4,12,64]{2,1,0:T(8,128)S(1)} %get-tuple-element.31), kind=kOutput, calls=%fused_computation.19 | convolution fusion | flops 25755648 | bytes 1585152 | tf_op jit(solution)/shard_map/chij,ichd->jchd/dot_general | solution.py:32
  113.4 2.0 pad_maximum_fusion
  115.4 4.1 %copy.207 = bf16[64,4,3,12,64]{4,3,2,1,0:T(8,128)(2,1)S(1)} copy(bf16[64,4,3,12,64]{0,4,3,1,2:T(8,128)(2,1)} %pad_maximum_fusion) | data formatting | bytes 2359296 | tf_op jit(solution)/shard_map/stack | solution.py:44
  119.6 2.8 %reshape.78 = bf16[256,2304]{1,0:T(8,128)(2,1)} reshape(bf16[64,4,3,12,64]{4,3,2,1,0:T(8,128)(2,1)S(1)} %copy.207) | data formatting | bytes 2359296 | tf_op jit(solution)/shard_map/reshape | solution.py:44
  122.3 3.6 %fusion.12 = bf16[256,768]{1,0:T(8,128)(2,1)S(1)} fusion(f32[256,768]{1,0:T(8,128)} %reshape.86, bf16[256,2304]{1,0:T(8,128)(2,1)} %reshape.78, bf16[768,2304]{0,1:T(8,128)(2,1)} %all-gather.2.cloned.1.call-done), kind=kOutput, calls=%fused_computation.21 | convolution fusion | flops 906362880 | bytes 5898240 | tf_op jit(solution)/shard_map/dot_general | solution.py:78
  126.9 16.1 %all-to-all-start.2 = ((bf16[64,4,768]{2,1,0:T(4,128)(2,1)}), bf16[64,4,768]{2,1,0:T(4,128)(2,1)S(1)}, u32[]{:S(2)}, u32[]{:S(2)}) async-start(bf16[64,4,768]{2,1,0:T(4,128)(2,1)} %reshape.79), calls=%async_computation.2 | async-start | bytes 786432 | tf_op jit(solution)/shard_map/all_to_all | solution.py:82
  144.3 8.8 %all-to-all-done.2 = bf16[64,4,768]{2,1,0:T(4,128)(2,1)S(1)} async-done(((bf16[64,4,768]{2,1,0:T(4,128)(2,1)}), bf16[64,4,768]{2,1,0:T(4,128)(2,1)S(1)}, u32[]{:S(2)}, u32[]{:S(2)}) %all-to-all-start.2) | async-done | bytes 393248 | tf_op jit(solution)/shard_map/all_to_all | solution.py:82
  154.9 1.0 copy.278
  156.0 3.9 %all-to-all-start.3 = ((f32[32,12,4,128]{3,2,1,0:T(4,128)}), f32[32,12,4,128]{3,2,1,0:T(4,128)S(1)}, u32[]{:S(2)}, u32[]{:S(2)}) async-start(f32[32,12,4,128]{3,2,1,0:T(4,128)} %bitcast.122), calls=%async_computation.3 | async-start | bytes 1572864 | tf_op jit(solution)/shard_map/all_to_all | solution.py:54
  159.9 2.9 %fusion.22 = f32[4,12,64,64]{3,2,1,0:T(8,128)} fusion(bf16[64,4,1,12,64]{0,4,3,1,2:T(8,128)(2,1)S(1)} %copy-done.8, f32[4,12,64,64]{2,3,1,0:T(8,128)} %get-tuple-element.32, f32[4,12,64]{2,1,0:T(8,128)S(1)} %copy-done.18), kind=kOutput, calls=%fused_computation.34 | convolution fusion | flops 25559040 | bytes 1978368 | tf_op jit(solution)/shard_map/chij,jchd->ichd/dot_general | solution.py:28
  162.8 1.9 copy.197
  167.0 7.2 %all-to-all-done.3 = f32[32,12,4,128]{3,2,1,0:T(4,128)S(1)} async-done(((f32[32,12,4,128]{3,2,1,0:T(4,128)}), f32[32,12,4,128]{3,2,1,0:T(4,128)S(1)}, u32[]{:S(2)}, u32[]{:S(2)}) %all-to-all-start.3) | async-done | bytes 786464 | tf_op jit(solution)/shard_map/all_to_all | solution.py:54
  174.7 22.9 %all_gather.11 = bf16[12,128,128]{2,0,1:T(8,128)(2,1)S(1)} all-gather(bf16[12,4,128]{2,0,1:T(8,128)(2,1)S(1)} %copy.212), channel_id=1, replica_groups=mesh['grp'=16,'seq'=32] {'seq'}, dimensions={1}, use_global_device_ids=true | all-gather | bytes 405504 | tf_op jit(solution)/shard_map/all_gather | solution.py:93
  (77 shorter events, 14.2 us)
Async XLA Ops:
  7.2 76.8 %all-gather.2.cloned.1.call-start = ((), (), s32[]{:S(2)}) async-start(), calls=%async_computation.4 | async-start | bytes 3760128 | tf_op jit(solution)/shard_map/all_gather | solution.py:74
  9.1 2.7 %copy-start.2 = (bf16[2,128,768]{1,2,0:T(8,128)(2,1)}, bf16[2,128,768]{1,2,0:T(8,128)(2,1)S(1)}, u32[]{:S(2)}) copy-start(bf16[2,128,768]{1,2,0:T(8,128)(2,1)S(1)} %copy.181) | copy-start | bytes 1179652
  10.5 1.4 copy-start
  10.8 11.5 %copy-start.14 = (bf16[2,128,768]{2,1,0:T(8,128)(2,1)S(1)}, bf16[2,128,768]{2,1,0:T(8,128)(2,1)}, u32[]{:S(2)}) copy-start(bf16[2,128,768]{2,1,0:T(8,128)(2,1)} %param.7) | copy-start | bytes 1179652
  11.9 24.8 %all-to-all-start = ((f32[32,12,4,128]{3,2,1,0:T(4,128)}), f32[32,12,4,128]{3,2,1,0:T(4,128)S(1)}, u32[]{:S(2)}, u32[]{:S(2)}) async-start(f32[32,12,4,128]{3,2,1,0:T(4,128)} %bitcast.123), calls=%async_computation | async-start | bytes 1572864 | tf_op jit(solution)/shard_map/all_to_all | solution.py:54
  37.0 23.4 %copy-start.15 = (f32[12,4,128]{2,1,0:T(4,128)}, f32[12,4,128]{2,1,0:T(4,128)S(1)}, u32[]{:S(2)}) copy-start(f32[12,4,128]{2,1,0:T(4,128)S(1)} %get-tuple-element.30) | copy-start | bytes 73732
  60.0 0.8 copy-start.4
  60.4 6.4 %copy-start.11 = (bf16[64,4,768]{2,1,0:T(4,128)(2,1)S(1)}, bf16[64,4,768]{2,1,0:T(4,128)(2,1)}, u32[]{:S(2)}) copy-start(bf16[64,4,768]{2,1,0:T(4,128)(2,1)} %param.9) | copy-start | bytes 1179652
  61.8 15.1 %all-to-all-start.1 = ((bf16[2,128,768]{2,0,1:T(2,128)(2,1)}), bf16[2,128,768]{2,0,1:T(2,128)(2,1)S(1)}, u32[]{:S(2)}, u32[]{:S(2)}) async-start(bf16[2,128,768]{2,0,1:T(2,128)(2,1)} %copy.189), calls=%async_computation.1 | async-start | bytes 786432 | tf_op jit(solution)/shard_map/all_to_all | solution.py:71
  93.7 2.1 %copy-start.12 = (bf16[64,4,1,12,64]{4,3,2,1,0:T(8,128)(2,1)S(1)}, bf16[64,4,1,12,64]{4,3,2,1,0:T(8,128)(2,1)}, u32[]{:S(2)}) copy-start(bf16[64,4,1,12,64]{4,3,2,1,0:T(8,128)(2,1)} %get-tuple-element.26) | copy-start | bytes 1179652
  95.8 4.2 %copy-start.7 = (bf16[64,4,1,12,64]{0,4,3,1,2:T(8,128)(2,1)}, bf16[64,4,1,12,64]{0,4,3,1,2:T(8,128)(2,1)S(1)}, u32[]{:S(2)}) copy-start(bf16[64,4,1,12,64]{0,4,3,1,2:T(8,128)(2,1)S(1)} %copy.238) | copy-start | bytes 1179652
  95.8 4.2 %copy-start.6 = (bf16[64,4,12,64]{3,2,1,0:T(8,128)(2,1)S(1)}, bf16[64,4,12,64]{3,2,1,0:T(8,128)(2,1)}, u32[]{:S(2)}) copy-start(bf16[64,4,12,64]{3,2,1,0:T(8,128)(2,1)} %reshape.96) | copy-start | bytes 1179652
  100.0 11.2 %copy-start.17 = (f32[4,12,64]{2,1,0:T(8,128)}, f32[4,12,64]{2,1,0:T(8,128)S(1)}, u32[]{:S(2)}) copy-start(f32[4,12,64]{2,1,0:T(8,128)S(1)} %get-tuple-element.31) | copy-start | bytes 36868
  111.1 2.3 %copy-start.13 = (bf16[64,4,1,12,64]{0,4,3,1,2:T(8,128)(2,1)S(1)}, bf16[64,4,1,12,64]{0,4,3,1,2:T(8,128)(2,1)}, u32[]{:S(2)}) copy-start(bf16[64,4,1,12,64]{0,4,3,1,2:T(8,128)(2,1)} %fusion.10) | copy-start | bytes 1179652
  126.0 17.0 %copy-start.3 = (bf16[2,128,768]{1,2,0:T(8,128)(2,1)S(1)}, bf16[2,128,768]{1,2,0:T(8,128)(2,1)}, u32[]{:S(2)}) copy-start(bf16[2,128,768]{1,2,0:T(8,128)(2,1)} %copy-done.2) | copy-start | bytes 1179652
  126.0 17.8 %copy-start.1 = (bf16[2,128,768]{1,2,0:T(8,128)(2,1)S(1)}, bf16[2,128,768]{1,2,0:T(8,128)(2,1)}, u32[]{:S(2)}) copy-start(bf16[2,128,768]{1,2,0:T(8,128)(2,1)} %copy-done) | copy-start | bytes 1179652
  126.0 17.8 %copy-start.9 = (f32[32,2,4,768]{3,0,2,1:T(8,128)S(1)}, f32[32,2,4,768]{3,0,2,1:T(8,128)}, u32[]{:S(2)}) copy-start(f32[32,2,4,768]{3,0,2,1:T(8,128)} %get-tuple-element.27) | copy-start | bytes 2359300
  126.9 26.3 %all-to-all-start.2 = ((bf16[64,4,768]{2,1,0:T(4,128)(2,1)}), bf16[64,4,768]{2,1,0:T(4,128)(2,1)S(1)}, u32[]{:S(2)}, u32[]{:S(2)}) async-start(bf16[64,4,768]{2,1,0:T(4,128)(2,1)} %reshape.79), calls=%async_computation.2 | async-start | bytes 786432 | tf_op jit(solution)/shard_map/all_to_all | solution.py:82
  154.9 5.0 %copy-start.8 = (bf16[64,4,1,12,64]{0,4,3,1,2:T(8,128)(2,1)S(1)}, bf16[64,4,1,12,64]{0,4,3,1,2:T(8,128)(2,1)}, u32[]{:S(2)}) copy-start(bf16[64,4,1,12,64]{0,4,3,1,2:T(8,128)(2,1)} %copy-done.7) | copy-start | bytes 1179652
  154.9 5.0 %copy-start.18 = (f32[4,12,64]{2,1,0:T(8,128)S(1)}, f32[4,12,64]{2,1,0:T(8,128)}, u32[]{:S(2)}) copy-start(f32[4,12,64]{2,1,0:T(8,128)} %copy-done.17) | copy-start | bytes 36868
  156.0 18.3 %all-to-all-start.3 = ((f32[32,12,4,128]{3,2,1,0:T(4,128)}), f32[32,12,4,128]{3,2,1,0:T(4,128)S(1)}, u32[]{:S(2)}, u32[]{:S(2)}) async-start(f32[32,12,4,128]{3,2,1,0:T(4,128)} %bitcast.122), calls=%async_computation.3 | async-start | bytes 1572864 | tf_op jit(solution)/shard_map/all_to_all | solution.py:54
  164.7 1.0 copy-start.5
  165.8 8.6 %copy-start.16 = (f32[12,4,128]{2,1,0:T(4,128)S(1)}, f32[12,4,128]{2,1,0:T(4,128)}, u32[]{:S(2)}) copy-start(f32[12,4,128]{2,1,0:T(4,128)} %copy-done.15) | copy-start | bytes 73732
  166.0 31.6 %copy-start.10 = (bf16[2,128,12,64]{1,3,0,2:T(8,128)(2,1)S(1)}, bf16[2,128,12,64]{1,3,0,2:T(8,128)(2,1)}, u32[]{:S(2)}) copy-start(bf16[2,128,12,64]{1,3,0,2:T(8,128)(2,1)} %copy.217) | copy-start | bytes 1179652
Sparse Core Ops, SparseCore 0:
  10.1 73.8 all-gather.1

commit v2 on v0

v2 whole, which is shorter than its diff:
```python
import functools
import math

import jax
import jax.numpy as jnp
from jax import lax
from jax.experimental import pallas as pl
from jax.experimental.pallas import tpu as pltpu
from jax.sharding import PartitionSpec as P

HEADS = 12
HEAD_DIM = 64
CHIPS = 16
SIDE = 4
HALF = 384
PAIRS = 3
MESH = pl.DeviceIdType.MESH
F32 = jnp.float32
BF16 = jnp.bfloat16

NN = (((1,), (0,)), ((), ()))
NT = (((1,), (1,)), ((), ()))
TN = (((0,), (0,)), ((), ()))


def dot(x, y, dims):
    return lax.dot_general(x, y, dims, preferred_element_type=F32)


def kernel(
    planes,
    q_in, k_in, v_in, w_in, cot_in,
    out, gq_out, gk_out, gv_out,
    qh, kh, vh, cot, weight, bias,
    s_send, s_recv, p_own, p_all, z_send, z_recv, abe, dabe, out_v,
    dz_send, dz_recv, dz_rows, g_send, g_recv, ds_all, gqh, gkh, gvh,
    local_sem, swap_send, swap_recv, ring_send, ring_recv, side_send, side_recv,
    s_ss, s_rs, p_ss, p_rs, z_ss, z_rs, dz_ss, dz_rs, g_ss, g_rs, ds_ss, ds_rs,
    back_send, back_recv,
):
    grp = lax.axis_index("grp")
    me = lax.axis_index("seq")
    chip = me // 2
    core = me % 2
    other = 1 - core
    chip_x, chip_y = chip % SIDE, chip // SIDE
    sibling = (grp, chip * 2 + other)
    above = (grp + 1) % planes
    below = (grp + planes - 1) % planes
    up_steps = planes // 2
    down_steps = (planes - 1) // 2
    scale = 1.0 / (math.sqrt(HEAD_DIM) * math.sqrt(4 * CHIPS))

    def target(k):
        return (chip_y + k // SIDE) % SIDE * SIDE + (chip_x + k % SIDE) % SIDE

    def source(k):
        return (chip_y + SIDE - k // SIDE) % SIDE * SIDE + (chip_x + SIDE - k % SIDE) % SIDE

    def remote(src, dst, send, recv, device):
        return pltpu.make_async_remote_copy(
            src_ref=src, dst_ref=dst, send_sem=send, recv_sem=recv,
            device_id=device, device_id_type=MESH,
        )

    barrier = pltpu.get_barrier_semaphore()

    @pl.loop(1, 2 * CHIPS)
    def _(k):
        pl.semaphore_signal(
            barrier, inc=1, device_id=(grp, (me + k) % (2 * CHIPS)), device_id_type=MESH
        )

    greeted = 2 * CHIPS - 1
    if up_steps:
        pl.semaphore_signal(barrier, inc=1, device_id=(above, me), device_id_type=MESH)
        pl.semaphore_signal(barrier, inc=1, device_id=(below, me), device_id_type=MESH)
        greeted += 2
    pl.semaphore_wait(barrier, greeted)

    mine = pl.ds(pl.multiple_of(core * HALF, HALF), HALF)
    theirs = pl.ds(pl.multiple_of(other * HALF, HALF), HALF)
    own_rows = pl.ds(core * 2, 2)
    their_rows = pl.ds(other * 2, 2)
    swaps, locals_ = [], []
    for n, (src, dst) in enumerate(((q_in, qh), (k_in, kh), (v_in, vh))):
        swaps.append(
            remote(src.at[:, :, theirs], dst.at[own_rows], swap_send.at[n], swap_recv.at[n], sibling)
        )
        locals_.append(
            pltpu.make_async_copy(src.at[:, :, mine], dst.at[own_rows], local_sem.at[n])
        )
    for n in range(3):
        swaps[n].start()
        locals_[n].start()

    def up_copy(step):
        block = (grp + planes - step) % planes
        src = w_in.at[:, mine] if step == 0 else weight.at[core, block]
        return remote(
            src, weight.at[core, block], ring_send.at[0, step], ring_recv.at[0, step], (above, me)
        )

    def down_copy(step):
        block = (grp + step) % planes
        src = w_in.at[:, mine] if step == 0 else weight.at[core, block]
        return remote(
            src, weight.at[core, block], ring_send.at[1, step], ring_recv.at[1, step], (below, me)
        )

    def side_copy(way, step):
        block = (grp + planes - step) % planes if way == 0 else (grp + step) % planes
        return remote(
            weight.at[core, block], weight.at[core, block],
            side_send.at[way, step], side_recv.at[way, step], sibling,
        )

    if up_steps:
        up_copy(0).start()
    if down_steps:
        down_copy(0).start()
    weight_own = [
        pltpu.make_async_copy(
            w_in.at[:, pl.ds(half * HALF, HALF)], weight.at[half, grp], local_sem.at[3 + half]
        )
        for half in range(2)
    ]
    for copy in weight_own:
        copy.start()
    cot_copy = pltpu.make_async_copy(cot_in, cot, local_sem.at[5])
    cot_copy.start()

    def ring(step):
        if step <= up_steps:
            up_copy(step - 1).wait_recv()
            if step < up_steps:
                up_copy(step).start()
            side_copy(0, step).start()
        if step <= down_steps:
            down_copy(step - 1).wait_recv()
            if step < down_steps:
                down_copy(step).start()
            side_copy(1, step).start()

    lane = lax.broadcasted_iota(jnp.int32, (1, 128), 1)
    low = jnp.where(lane < HEAD_DIM, 1.0, 0.0).astype(BF16)
    high = jnp.where(lane < HEAD_DIM, 0.0, 1.0).astype(BF16)
    low4 = jnp.concatenate([low] * 4, axis=1)
    high4 = jnp.concatenate([high] * 4, axis=1)
    row_id = lax.broadcasted_iota(jnp.int32, (256, 256), 0)
    col_id = lax.broadcasted_iota(jnp.int32, (256, 256), 1)
    bias[...] = jnp.where(row_id % 4 == col_id % 4, 0.0, -1e30)

    def wide(ref, t):
        return jnp.concatenate([ref[r, :, 128 * t : 128 * t + 128] for r in range(4)], axis=1)

    def terms(left, right, send_ref, t):
        for e, keep in enumerate((low4, high4)):
            h = 2 * t + e
            part = dot(left, right * keep, NT)
            send_ref[8 * (h // 3) : 8 * (h // 3) + 8, h % 3] = part.reshape(8, 16, 128)

    def gathered(ref, h):
        return ref[8 * (h // 3) : 8 * (h // 3) + 8, h % 3].reshape(128, 128)

    def scatter_copy(send_ref, recv_ref, ss, rs, to, slot):
        return remote(send_ref.at[to], recv_ref.at[slot], ss.at[to], rs.at[slot], (grp, to * 2 + core))

    def scatter_start(send_ref, recv_ref, ss, rs):
        @pl.loop(1, CHIPS)
        def _(k):
            scatter_copy(send_ref, recv_ref, ss, rs, target(k), chip).start()
        recv_ref[chip] = send_ref[chip]

    def scatter_wait(send_ref, recv_ref, ss, rs, first, last):
        @pl.loop(first, last)
        def _(k):
            scatter_copy(send_ref, recv_ref, ss, rs, target(k), source(k)).wait_recv()

    def gather_copy(ref, ss, rs, to, slot):
        return remote(ref.at[slot], ref.at[slot], ss.at[to], rs.at[slot], (grp, to * 2 + core))

    def gather_start(ref, ss, rs):
        @pl.loop(1, CHIPS)
        def _(k):
            gather_copy(ref, ss, rs, target(k), chip).start()

    def gather_wait(ref, ss, rs):
        @pl.loop(1, CHIPS)
        def _(k):
            gather_copy(ref, ss, rs, target(k), source(k)).wait_recv()

    for n in range(2):
        swaps[n].wait_recv()
        locals_[n].wait()
    for t in range(PAIRS):
        terms(wide(qh, t), wide(kh, t), s_send, t)
    scatter_start(s_send, s_recv, s_ss, s_rs)
    ring(1)
    scatter_wait(s_send, s_recv, s_ss, s_rs, 1, 8)
    ring(2)
    scatter_wait(s_send, s_recv, s_ss, s_rs, 8, CHIPS)
    scores = jnp.sum(s_recv[...], axis=0) * scale
    shifted = jnp.exp(scores - jnp.max(scores, axis=-1, keepdims=True))
    probs = shifted / jnp.sum(shifted, axis=-1, keepdims=True)
    p_own[...] = probs
    p_all[chip] = probs.astype(BF16)
    gather_start(p_all, p_ss, p_rs)
    ring(3)
    swaps[2].wait_recv()
    locals_[2].wait()
    gather_wait(p_all, p_ss, p_rs)
    ring(4)

    first4 = lax.broadcasted_iota(jnp.int32, (16, 8, 128), 1) < 4

    def interleave(x, y):
        lo = jnp.where(first4, x, pltpu.roll(y, 4, 1))
        hi = jnp.where(first4, pltpu.roll(x, 4, 1), y)
        return lo, hi

    for t in range(PAIRS):
        values = wide(vh, t)
        z = dot(gathered(p_all, 2 * t), values * low4, NN) + dot(
            gathered(p_all, 2 * t + 1), values * high4, NN
        )
        rows = [z[:, 128 * r : 128 * r + 128].reshape(16, 8, 128) for r in range(4)]
        lo01, hi01 = interleave(rows[0], rows[1])
        lo23, hi23 = interleave(rows[2], rows[3])
        lanes = slice(128 * t, 128 * t + 128)
        z_send[:, 0, :, lanes] = jnp.concatenate([lo01, lo23], axis=1).astype(BF16)
        z_send[:, 1, :, lanes] = jnp.concatenate([hi01, hi23], axis=1).astype(BF16)

    def z_copy(to, to_core, slot_core, slot):
        return remote(
            z_send.at[to, to_core], z_recv.at[slot_core, slot],
            z_ss.at[to, to_core], z_rs.at[slot_core, slot], (grp, to * 2 + to_core),
        )

    @pl.loop(1, CHIPS)
    def _(k):
        z_copy(target(k), core, core, chip).start()
        z_copy(target(k), other, core, chip).start()
    z_copy(chip, other, core, chip).start()
    z_recv[core, chip] = z_send[chip, core]

    for step in range(5, up_steps + 1):
        ring(step)

    for copy in weight_own:
        copy.wait()
    for step in range(1, up_steps + 1):
        side_copy(0, step).wait_recv()
    for step in range(1, down_steps + 1):
        side_copy(1, step).wait_recv()
    cot_copy.wait()

    z_copy(chip, other, other, chip).wait_recv()

    @pl.loop(1, CHIPS)
    def _(k):
        z_copy(target(k), core, core, source(k)).wait_recv()
        z_copy(target(k), other, other, source(k)).wait_recv()

    z0 = z_recv[0].reshape(256, HALF)
    z1 = z_recv[1].reshape(256, HALF)
    share = weight.shape[2]
    channels = planes * share
    for part in range(3):
        lo, hi = part * 768, part * 768 + 768
        w0 = weight[0].reshape(channels, HALF)[lo:hi]
        w1 = weight[1].reshape(channels, HALF)[lo:hi]
        packed = (dot(z0, w0, NT) + dot(z1, w1, NT)).astype(BF16)
        for u in range(6):
            abe[6 * part + u] = packed[:, 128 * u : 128 * u + 128]

    @pl.loop(0, 6)
    def _(u):
        lanes = pl.ds(pl.multiple_of(u * 128, 128), 128)
        half_lanes = pl.ds(pl.multiple_of((u % 3) * 128, 128), 128)
        a, b, e = abe[u], abe[6 + u], abe[12 + u]
        g = cot[:, lanes]
        att = z_recv[u // 3, :, :, half_lanes].reshape(256, 128).astype(F32)
        da = db = dc = None
        for keep in (low, high):
            ak, bk, ek, gk = a * keep, b * keep, e * keep, g * keep
            logits = dot(a, bk, NT) * 0.125 + bias[...]
            shifted = jnp.exp(logits - jnp.max(logits, axis=-1, keepdims=True))
            weights = shifted * (1.0 / jnp.sum(shifted, axis=-1, keepdims=True))
            weights_low = weights.astype(BF16)
            slope = dot(g, ek, NT)
            mean = jnp.sum(weights * slope, axis=-1, keepdims=True)
            dlogits = (weights * (slope - mean) * 0.125).astype(BF16)
            att = att + dot(weights_low, ek, NN)
            terms_ = (dot(dlogits, bk, NN), dot(dlogits, ak, TN), dot(weights_low, gk, TN))
            if da is None:
                da, db, dc = terms_
            else:
                da, db, dc = da + terms_[0], db + terms_[1], dc + terms_[2]
        out_v[:, lanes] = att.astype(BF16)
        dabe[u] = da.astype(BF16)
        dabe[6 + u] = db.astype(BF16)
        dabe[12 + u] = dc.astype(BF16)

    out_copy = pltpu.make_async_copy(out_v, out, local_sem.at[6])
    out_copy.start()

    def dz_copy(to, to_core, slot, slot_core):
        return remote(
            dz_send.at[to_core, to], dz_recv.at[slot, slot_core],
            dz_ss.at[to_core, to], dz_rs.at[slot, slot_core], (grp, to * 2 + to_core),
        )

    dpacked = jnp.concatenate([dabe[n] for n in range(18)], axis=1)
    for half in range(2):
        back = cot[:, half * HALF : half * HALF + HALF].astype(F32) + dot(
            dpacked, weight[half].reshape(channels, HALF), NN
        )
        dz_send[half] = back.astype(BF16).reshape(16, 16, HALF)

    @pl.loop(1, CHIPS)
    def _(k):
        dz_copy(target(k), core, chip, core).start()
        dz_copy(target(k), other, chip, core).start()
    dz_copy(chip, other, chip, core).start()
    dz_recv[chip, core] = dz_send[core, chip]

    dz_copy(chip, other, chip, other).wait_recv()

    @pl.loop(1, CHIPS)
    def _(k):
        dz_copy(target(k), core, source(k), core).wait_recv()
        dz_copy(target(k), other, source(k), other).wait_recv()

    for t in range(PAIRS):
        lanes = slice(128 * t, 128 * t + 128)
        even = dz_recv[:, 0, :, lanes].astype(F32)
        odd = dz_recv[:, 1, :, lanes].astype(F32)
        r0, r1 = interleave(even[:, :8], odd[:, :8])
        r2, r3 = interleave(even[:, 8:], odd[:, 8:])
        dz = jnp.concatenate(
            [x.reshape(128, 128).astype(BF16) for x in (r0, r1, r2, r3)], axis=1
        )
        dz_rows[t] = dz
        terms(dz, wide(vh, t), g_send, t)
    scatter_start(g_send, g_recv, g_ss, g_rs)

    def store(ref, t, x):
        for r in range(4):
            ref[r, :, 128 * t : 128 * t + 128] = x[:, 128 * r : 128 * r + 128].astype(BF16)

    def give_back(ref, out_ref, n):
        local = pltpu.make_async_copy(ref.at[own_rows], out_ref.at[:, :, mine], local_sem.at[7 + n])
        away = remote(
            ref.at[their_rows], out_ref.at[:, :, mine], back_send.at[n], back_recv.at[n], sibling
        )
        landing = remote(
            ref.at[their_rows], out_ref.at[:, :, theirs], back_send.at[n], back_recv.at[n], sibling
        )
        local.start()
        away.start()
        return local, away, landing

    for t in range(PAIRS):
        dz = dz_rows[t]
        store(gvh, t, dot(gathered(p_all, 2 * t), dz * low4, TN)
              + dot(gathered(p_all, 2 * t + 1), dz * high4, TN))
    returned = [give_back(gvh, gv_out, 0)]

    scatter_wait(g_send, g_recv, g_ss, g_rs, 1, CHIPS)
    slope = jnp.sum(g_recv[...], axis=0)
    probs = p_own[...]
    mean = jnp.sum(probs * slope, axis=-1, keepdims=True)
    ds_all[chip] = (probs * (slope - mean) * scale).astype(BF16)
    gather_start(ds_all, ds_ss, ds_rs)
    gather_wait(ds_all, ds_ss, ds_rs)
    for t in range(PAIRS):
        keys = wide(kh, t)
        store(gqh, t, dot(gathered(ds_all, 2 * t), keys * low4, NN)
              + dot(gathered(ds_all, 2 * t + 1), keys * high4, NN))
    returned.append(give_back(gqh, gq_out, 1))
    for t in range(PAIRS):
        query = wide(qh, t)
        store(gkh, t, dot(gathered(ds_all, 2 * t), query * low4, TN)
              + dot(gathered(ds_all, 2 * t + 1), query * high4, TN))
    returned.append(give_back(gkh, gk_out, 2))

    for copy in swaps:
        copy.wait_send()
    for step in range(up_steps):
        up_copy(step).wait_send()
        side_copy(0, step + 1).wait_send()
    for step in range(down_steps):
        down_copy(step).wait_send()
        side_copy(1, step + 1).wait_send()

    @pl.loop(1, CHIPS)
    def _(k):
        to = target(k)
        scatter_copy(s_send, s_recv, s_ss, s_rs, to, chip).wait_send()
        gather_copy(p_all, p_ss, p_rs, to, chip).wait_send()
        z_copy(to, core, core, chip).wait_send()
        z_copy(to, other, core, chip).wait_send()
        dz_copy(to, core, chip, core).wait_send()
        dz_copy(to, other, chip, core).wait_send()
        scatter_copy(g_send, g_recv, g_ss, g_rs, to, chip).wait_send()
        gather_copy(ds_all, ds_ss, ds_rs, to, chip).wait_send()
    z_copy(chip, other, core, chip).wait_send()
    dz_copy(chip, other, chip, core).wait_send()
    out_copy.wait()
    for local, away, landing in returned:
        local.wait()
        away.wait_send()
        landing.wait_recv()


def on_device(planes, row_query, row_key, row_value, column_weight, cotangent):
    own_rows, columns, width = row_query.shape
    share = column_weight.shape[1]
    rows, own_columns, _ = cotangent.shape
    vmem = pltpu.VMEM
    sem = pltpu.SemaphoreType.DMA
    row_shape = jax.ShapeDtypeStruct((own_rows, columns, width), BF16)
    column_output, grad_query, grad_key, grad_value = pl.pallas_call(
        functools.partial(kernel, planes),
        out_shape=(
            jax.ShapeDtypeStruct((rows * own_columns, width), BF16),
            row_shape, row_shape, row_shape,
        ),
        in_specs=[pl.BlockSpec(memory_space=pl.ANY)] * 5,
        out_specs=[pl.BlockSpec(memory_space=pl.ANY)] * 4,
        scratch_shapes=[
            vmem((4, 128, HALF), BF16),
            vmem((4, 128, HALF), BF16),
            vmem((4, 128, HALF), BF16),
            vmem((256, 768), BF16),
            vmem((2, planes, share, HALF), BF16),
            vmem((256, 256), F32),
            vmem((CHIPS, 3, 16, 128), F32),
            vmem((CHIPS, 3, 16, 128), F32),
            vmem((3, 16, 128), F32),
            vmem((CHIPS, 3, 16, 128), BF16),
            vmem((CHIPS, 2, 16, HALF), BF16),
            vmem((2, CHIPS, 16, HALF), BF16),
            vmem((18, 256, 128), BF16),
            vmem((18, 256, 128), BF16),
            vmem((256, 768), BF16),
            vmem((2, CHIPS, 16, HALF), BF16),
            vmem((CHIPS, 2, 16, HALF), BF16),
            vmem((PAIRS, 128, 512), BF16),
            vmem((CHIPS, 3, 16, 128), F32),
            vmem((CHIPS, 3, 16, 128), F32),
            vmem((CHIPS, 3, 16, 128), BF16),
            vmem((4, 128, HALF), BF16),
            vmem((4, 128, HALF), BF16),
            vmem((4, 128, HALF), BF16),
            sem((10,)),
            sem((3,)), sem((3,)),
            sem((2, planes)), sem((2, planes)),
            sem((2, planes)), sem((2, planes)),
            sem((CHIPS,)), sem((CHIPS,)),
            sem((CHIPS,)), sem((CHIPS,)),
            sem((CHIPS, 2)), sem((2, CHIPS)),
            sem((2, CHIPS)), sem((CHIPS, 2)),
            sem((CHIPS,)), sem((CHIPS,)),
            sem((CHIPS,)), sem((CHIPS,)),
            sem((3,)), sem((3,)),
        ],
        compiler_params=pltpu.CompilerParams(
            collective_id=0, has_side_effects=True, vmem_limit_bytes=48 * 1024 * 1024
        ),
    )(
        row_query, row_key, row_value, column_weight.T,
        cotangent.reshape(rows * own_columns, width),
    )
    return (
        column_output.reshape(rows, own_columns, width), grad_query, grad_key, grad_value
    )


def solution(mesh):
    planes = mesh.shape["grp"]
    in_specs = (
        P(("grp", "seq"), None, None),
        P(("grp", "seq"), None, None),
        P(("grp", "seq"), None, None),
        P(None, "grp"),
        P("grp", "seq", None),
    )
    out_specs = (
        P("grp", "seq", None),
        P(("grp", "seq"), None, None),
        P(("grp", "seq"), None, None),
        P(("grp", "seq"), None, None),
    )
    return jax.shard_map(
        functools.partial(on_device, planes),
        mesh=mesh, in_specs=in_specs, out_specs=out_specs, check_vma=False,
    )
```

time: 400 us -> 95.7 us (0.24)
  waiting for transfers between devices: 279 us -> 0 us
  Pallas kernels: 0 us -> 88.6 us
  matrix products: 57.3 us -> 0 us
  local copies, waits for them, and re-layouts: 30.5 us -> 6.21 us
  between operations: 15.9 us -> 0.67 us
  starting transfers between devices: 10.1 us -> 0 us
  other arithmetic: 6.57 us -> 0 us
    psum x2 -> x0, waiting for transfers between devices: 266 us -> none  [the longest x1 140 us: on_device(): probs = softmax_rows(lax.psum(local_scores, 'seq') * scale)]
    pallas_call x0 -> x1, Pallas kernels: none -> 88.6 us  [on_device(): pl.pallas_call(functools.partial(kernel, planes), out_shape=(jax.ShapeDty...]
    dot_general x10 -> x0, matrix products: 29 us -> none  [the longest x1 4.92 us: column_pass(): jnp.einsum('chij,ichd->jchd', grad_logits, query, preferred_element_type=...]
    unnamed x3 -> x0, matrix products: 24.1 us -> none
    reshape x12 -> x2, local copies, waits for them, and re-layouts: 14.5 us -> 2 us  [the longest x1 1.16 us: on_device(): cotangent.reshape(rows * own_columns, width)]
    all_to_all x2 -> x0, waiting for transfers between devices: 12.1 us -> none  [the longest x1 7.61 us: on_device(): lax.all_to_all(hidden, 'seq', split_axis=1, concat_axis=0, tiled=True)]
    all_to_all x2 -> x0, starting transfers between devices: 9.71 us -> none  [the longest x1 5.82 us: on_device(): lax.all_to_all(hidden, 'seq', split_axis=1, concat_axis=0, tiled=True)]
    sub x1 -> x0, matrix products: 4.18 us -> none  [softmax_rows(): shifted = jnp.exp(logits - jnp.max(logits, axis=-1, keepdims=True))]
  transfers between devices with their start and end apart: 5 -> 0, of which waited for: 4 -> 0; matrix products, arithmetic and copies ran while one was open for 6% -> 0% of each run, Pallas kernels for 0% -> 0%
where the time goes in v2:
time: 95.7 us; the launch traced here: 95.4 us
  Pallas kernels  88.6 us (93%)
  local copies, waits for them, and re-layouts  6.21 us (6%)
    pallas_call x1, Pallas kernels, on_device(): pl.pallas_call(functools.partial(kernel, planes), out_shape=(jax.ShapeDty...  88.6 us
    unnamed x11, local copies, waits for them, and re-layouts  4.21 us

profile of v2, /device:TPU:1, one launch (start us, length us, event | category | flops | bytes accessed | tf_op | source)
XLA Modules:
  0.0 95.4 jit_solution(14418034128257822926)
XLA Ops:
  0.6 0.0 copy-start
  0.6 0.0 copy-start.1
  0.7 1.2 %reshape.14.cot_in = bf16[256,768]{1,0:T(8,128)(2,1)S(1)} reshape(bf16[64,4,768]{2,1,0:T(4,128)(2,1)} %param.9) | data formatting | bytes 786432 | tf_op jit(solution)/shard_map/reshape | solution.py:474
  1.8 0.0 copy-done
  1.8 0.0 copy-done.1
  1.9 0.0 copy-start.2
  1.9 1.0 %copy-done.2 = bf16[2,128,768]{2,1,0:T(8,128)(2,1)S(1)} copy-done((bf16[2,128,768]{2,1,0:T(8,128)(2,1)S(1)}, bf16[2,128,768]{2,1,0:T(8,128)(2,1)}, u32[]{:S(2)}) %copy-start.2) | copy-done | bytes 393240
  2.9 0.0 copy-start.3
  2.9 0.9 copy-done.3
  3.8 88.6 %shard_map.84 = (bf16[256,768]{1,0:T(8,128)(2,1)S(1)}, bf16[2,128,768]{2,1,0:T(8,128)(2,1)S(1)}, bf16[2,128,768]{2,1,0:T(8,128)(2,1)S(1)}, bf16[2,128,768]{2,1,0:T(8,128)(2,1)S(1)}) custom-call(bf16[2,128,768]{2,1,0:T(8,128)(2,1)S(1)} %copy-done, bf16[2,128,768]{2,1,0:T(8,128)(2,1)S(1)} %copy-done.1, bf16[2,128,768]{2,1,0:T(8,128)(2,1)S(1)} %copy-done.2, ...), custom_call_target="tpu_custom_call" | custom-call | tf_op jit(solution)/shard_map/pallas_call | solution.py:424
  92.4 0.8 reshape.15
  93.2 0.7 copy.12
  93.9 0.7 copy.13
  94.7 0.7 copy.14
Async XLA Ops:
  0.6 1.2 %copy-start = (bf16[2,128,768]{2,1,0:T(8,128)(2,1)S(1)}, bf16[2,128,768]{2,1,0:T(8,128)(2,1)}, u32[]{:S(2)}) copy-start(bf16[2,128,768]{2,1,0:T(8,128)(2,1)} %q_in.1) | copy-start | bytes 1179652
  0.6 1.2 %copy-start.1 = (bf16[2,128,768]{2,1,0:T(8,128)(2,1)S(1)}, bf16[2,128,768]{2,1,0:T(8,128)(2,1)}, u32[]{:S(2)}) copy-start(bf16[2,128,768]{2,1,0:T(8,128)(2,1)} %k_in.1) | copy-start | bytes 1179652
  1.9 1.0 %copy-start.2 = (bf16[2,128,768]{2,1,0:T(8,128)(2,1)S(1)}, bf16[2,128,768]{2,1,0:T(8,128)(2,1)}, u32[]{:S(2)}) copy-start(bf16[2,128,768]{2,1,0:T(8,128)(2,1)} %v_in.1) | copy-start | bytes 1179652
  2.9 0.9 copy-start.3

commit v3 on v2

v3 whole, which is shorter than its diff:
```python
import functools
import math

import jax
import jax.numpy as jnp
from jax import lax
from jax.experimental import pallas as pl
from jax.experimental.pallas import tpu as pltpu
from jax.sharding import PartitionSpec as P

HEADS = 12
HEAD_DIM = 64
CHIPS = 16
SIDE = 4
HALF = 384
PAIRS = 3
MESH = pl.DeviceIdType.MESH
VMEM_LIMIT = 60 * 1024 * 1024
F32 = jnp.float32
BF16 = jnp.bfloat16

NN = (((1,), (0,)), ((), ()))
NT = (((1,), (1,)), ((), ()))
TN = (((0,), (0,)), ((), ()))


def dot(x, y, dims):
    return lax.dot_general(x, y, dims, preferred_element_type=F32)


def copy_out(*refs):
    sources, targets, sem = refs[:4], refs[4:8], refs[8]
    copies = [pltpu.make_async_copy(sources[n], targets[n], sem.at[n]) for n in range(4)]
    for copy in copies:
        copy.start()
    for copy in copies:
        copy.wait()


def kernel(
    planes,
    q_in, k_in, v_in, w_in, cot_in,
    out, gq_out, gk_out, gv_out,
    qh, kh, vh, cot4, cot, weight, bias,
    s_send, s_recv, p_own, p_all, z_send, z_recv, zh, abe, dabe, outh, out4,
    dz_send, dz_recv, dz_rows, g_send, g_recv, ds_all, gqh, gkh, gvh,
    local_sem, swap_send, swap_recv, ring_send, ring_recv, side_send, side_recv,
    many_send, many_recv, back_send, back_recv,
):
    grp = lax.axis_index("grp")
    me = lax.axis_index("seq")
    chip = lax.div(me, 2)
    core = lax.rem(me, 2)
    other = 1 - core
    chip_x, chip_y = lax.rem(chip, SIDE), lax.div(chip, SIDE)
    sibling = (grp, chip * 2 + other)
    above = lax.rem(grp + 1, planes)
    below = lax.rem(grp + planes - 1, planes)
    up_steps = planes // 2
    down_steps = (planes - 1) // 2
    scale = 1.0 / (math.sqrt(HEAD_DIM) * math.sqrt(4 * CHIPS))

    targets = [None] + [
        lax.rem(chip_y + k // SIDE, SIDE) * SIDE + lax.rem(chip_x + k % SIDE, SIDE)
        for k in range(1, CHIPS)
    ]

    def remote(src, dst, send, recv, device):
        return pltpu.make_async_remote_copy(
            src_ref=src, dst_ref=dst, send_sem=send, recv_sem=recv,
            device_id=device, device_id_type=MESH,
        )

    barrier = pltpu.get_barrier_semaphore()

    @pl.loop(1, 2 * CHIPS)
    def _(k):
        pl.semaphore_signal(
            barrier, inc=1, device_id=(grp, lax.rem(me + k, 2 * CHIPS)), device_id_type=MESH
        )

    greeted = 2 * CHIPS - 1
    if up_steps:
        pl.semaphore_signal(barrier, inc=1, device_id=(above, me), device_id_type=MESH)
        pl.semaphore_signal(barrier, inc=1, device_id=(below, me), device_id_type=MESH)
        greeted += 2
    pl.semaphore_wait(barrier, greeted)

    mine = pl.ds(pl.multiple_of(core * HALF, HALF), HALF)
    theirs = pl.ds(pl.multiple_of(other * HALF, HALF), HALF)
    own_rows = pl.ds(core * 2, 2)
    their_rows = pl.ds(other * 2, 2)
    swaps, locals_ = [], []
    for n, (src, dst) in enumerate(((q_in, qh), (k_in, kh), (v_in, vh))):
        swaps.append(
            remote(src.at[:, :, theirs], dst.at[own_rows], swap_send.at[n], swap_recv.at[n], sibling)
        )
        locals_.append(
            pltpu.make_async_copy(src.at[:, :, mine], dst.at[own_rows], local_sem.at[n])
        )
    for n in range(3):
        swaps[n].start()
        locals_[n].start()

    share = w_in.shape[0]
    first = (share // 16 + 1) // 2 * 16
    cuts = ((0, first), (first, share - first))

    def block_rows(way, step):
        block = lax.rem(grp + planes - step, planes) if way == 0 else lax.rem(grp + step, planes)
        return pl.multiple_of(block * share, 16)

    def ring_copy(way, step, part):
        begin, size = cuts[part]
        rows = pl.ds(pl.multiple_of(block_rows(way, step) + begin, 16), size)
        src = w_in.at[pl.ds(begin, size), mine] if step == 0 else weight.at[core, rows]
        return remote(
            src, weight.at[core, rows], ring_send.at[way, step, part],
            ring_recv.at[way, step, part], (below if way else above, me),
        )

    def side_copy(way, step):
        rows = weight.at[core, pl.ds(block_rows(way, step), share)]
        return remote(rows, rows, side_send.at[way, step], side_recv.at[way, step], sibling)

    for part in range(2):
        if up_steps:
            ring_copy(0, 0, part).start()
        if down_steps:
            ring_copy(1, 0, part).start()
    weight_own = [
        pltpu.make_async_copy(
            w_in.at[:, pl.ds(half * HALF, HALF)],
            weight.at[half, pl.ds(block_rows(0, 0), share)], local_sem.at[3 + half],
        )
        for half in range(2)
    ]
    for copy in weight_own:
        copy.start()
    cot_copy = pltpu.make_async_copy(cot_in, cot4, local_sem.at[5])
    cot_copy.start()

    def ring(first_turn, last_turn):
        for turn in range(first_turn, last_turn):
            step, part = turn // 2 + 1, turn % 2
            for way, steps in enumerate((up_steps, down_steps)):
                if step <= steps:
                    ring_copy(way, step - 1, part).wait_recv()
                    if step < steps:
                        ring_copy(way, step, part).start()
                    if part == 1:
                        side_copy(way, step).start()

    lane = lax.broadcasted_iota(jnp.int32, (1, 128), 1)
    low = jnp.where(lane < HEAD_DIM, 1.0, 0.0).astype(BF16)
    high = jnp.where(lane < HEAD_DIM, 0.0, 1.0).astype(BF16)
    low4 = jnp.concatenate([low] * 4, axis=1)
    high4 = jnp.concatenate([high] * 4, axis=1)
    row_id = lax.broadcasted_iota(jnp.int32, (128, 128), 0)
    col_id = lax.broadcasted_iota(jnp.int32, (128, 128), 1)
    bias[...] = jnp.where(row_id % 2 == col_id % 2, 0.0, -1e30)

    def wide(ref, t):
        return jnp.concatenate([ref[r, :, 128 * t : 128 * t + 128] for r in range(4)], axis=1)

    def terms(left, right, send_ref, t):
        for e, keep in enumerate((low4, high4)):
            h = 2 * t + e
            part = dot(left, right * keep, NT)
            send_ref[8 * (h // 3) : 8 * (h // 3) + 8, h % 3] = part.reshape(8, 16, 128)

    def gathered(ref, h):
        return ref[8 * (h // 3) : 8 * (h // 3) + 8, h % 3].reshape(128, 128)

    def scatter(send_ref, recv_ref, n):
        for k in range(1, CHIPS):
            to = targets[k]
            remote(
                send_ref.at[to], recv_ref.at[chip], many_send.at[n], many_recv.at[n],
                (grp, to * 2 + core),
            ).start()
        recv_ref[chip] = send_ref[chip]
        rest = pl.ds(0, CHIPS - 1)
        return remote(
            send_ref.at[rest], recv_ref.at[rest], many_send.at[n], many_recv.at[n], sibling
        )

    def gather(ref, n):
        for k in range(1, CHIPS):
            remote(
                ref.at[chip], ref.at[chip], many_send.at[n], many_recv.at[n],
                (grp, targets[k] * 2 + core),
            ).start()
        rest = pl.ds(0, CHIPS - 1)
        return remote(ref.at[rest], ref.at[rest], many_send.at[n], many_recv.at[n], sibling)

    def exchange(send_ref, recv_ref, n):
        for k in range(1, CHIPS):
            for to in (targets[k] * 2 + core, targets[k] * 2 + other):
                remote(
                    send_ref.at[to], recv_ref.at[me], many_send.at[n], many_recv.at[n], (grp, to)
                ).start()
        remote(
            send_ref.at[chip * 2 + other], recv_ref.at[me], many_send.at[n], many_recv.at[n],
            sibling,
        ).start()
        recv_ref[me] = send_ref[me]
        rest = pl.ds(0, 2 * CHIPS - 1)
        return remote(
            send_ref.at[rest], recv_ref.at[rest], many_send.at[n], many_recv.at[n], sibling
        )

    sublane = lax.broadcasted_iota(jnp.int32, (16, 8, 128), 1)
    first4 = sublane < 4
    first2 = lax.rem(sublane, 4) < 2

    def swap4(x, y):
        return jnp.where(first4, x, pltpu.roll(y, 4, 1)), jnp.where(first4, pltpu.roll(x, 4, 1), y)

    def swap2(x, y):
        return jnp.where(first2, x, pltpu.roll(y, 2, 1)), jnp.where(first2, pltpu.roll(x, 6, 1), y)

    for n in range(2):
        swaps[n].wait_recv()
        locals_[n].wait()
    for t in range(PAIRS):
        terms(wide(qh, t), wide(kh, t), s_send, t)
    s_all = scatter(s_send, s_recv, 0)
    ring(0, 3)
    s_all.wait_recv()
    scores = jnp.sum(s_recv[...], axis=0) * scale
    shifted = jnp.exp(scores - jnp.max(scores, axis=-1, keepdims=True))
    probs = shifted / jnp.sum(shifted, axis=-1, keepdims=True)
    p_own[...] = probs
    p_all[chip] = probs.astype(BF16)
    p_rest = gather(p_all, 1)
    ring(3, 6)
    cot_copy.wait()
    for u in range(6):
        lanes = slice(128 * u, 128 * u + 128)
        g4 = cot4[:, :, lanes].astype(F32)
        for c in range(2):
            cot[c, :, lanes] = g4[:, 2 * c : 2 * c + 2].reshape(128, 128).astype(BF16)
    swaps[2].wait_recv()
    locals_[2].wait()
    p_rest.wait_recv()

    for t in range(PAIRS):
        values = wide(vh, t)
        z = dot(gathered(p_all, 2 * t), values * low4, NN) + dot(
            gathered(p_all, 2 * t + 1), values * high4, NN
        )
        rows = [z[:, 128 * r : 128 * r + 128].reshape(16, 8, 128) for r in range(4)]
        lanes = slice(128 * t, 128 * t + 128)
        for c, (x, y) in enumerate(zip(swap4(rows[0], rows[2]), swap4(rows[1], rows[3]))):
            block = jnp.concatenate(swap2(x, y), axis=1).astype(BF16)
            for n in range(CHIPS):
                z_send[2 * n + c, :, lanes] = block[n]
    z_rest = exchange(z_send, z_recv, 2)
    ring(6, 2 * up_steps)

    for copy in weight_own:
        copy.wait()
    for step in range(1, up_steps + 1):
        side_copy(0, step).wait_recv()
    for step in range(1, down_steps + 1):
        side_copy(1, step).wait_recv()
    z_rest.wait_recv()

    arrived = z_recv[...].reshape(CHIPS, 2, 16, HALF)
    for half in range(2):
        for t in range(PAIRS):
            z = arrived[:, half, :, 128 * t : 128 * t + 128].astype(F32)
            lanes = slice(half * HALF + 128 * t, half * HALF + 128 * t + 128)
            for c in range(2):
                zh[128 * c : 128 * c + 128, lanes] = (
                    z[:, 8 * c : 8 * c + 8].reshape(128, 128).astype(BF16)
                )
    for part in range(3):
        rows = slice(part * 768, part * 768 + 768)
        w = jnp.concatenate([weight[0, rows], weight[1, rows]], axis=1)
        packed = dot(zh[...], w, NT).astype(BF16)
        for u in range(6):
            abe[6 * part + u] = packed[:, 128 * u : 128 * u + 128]

    @pl.loop(0, 6)
    def _(u):
        lanes = pl.ds(pl.multiple_of(u * 128, 128), 128)
        for c in range(2):
            rows = slice(128 * c, 128 * c + 128)
            a, b, e = abe[u, rows], abe[6 + u, rows], abe[12 + u, rows]
            g = cot[c, :, lanes]
            att = zh[rows, lanes].astype(F32)
            sums = None
            for keep in (low, high):
                ak, bk, ek, gk = a * keep, b * keep, e * keep, g * keep
                logits = dot(a, bk, NT) * 0.125 + bias[...]
                shifted = jnp.exp(logits - jnp.max(logits, axis=-1, keepdims=True))
                weights = shifted * (1.0 / jnp.sum(shifted, axis=-1, keepdims=True))
                weights_low = weights.astype(BF16)
                slope = dot(g, ek, NT)
                mean = jnp.sum(weights * slope, axis=-1, keepdims=True)
                dlogits = (weights * (slope - mean) * 0.125).astype(BF16)
                att = att + dot(weights_low, ek, NN)
                parts = (dot(dlogits, bk, NN), dot(dlogits, ak, TN), dot(weights_low, gk, TN))
                sums = parts if sums is None else [x + y for x, y in zip(sums, parts)]
            outh[c, :, lanes] = att.astype(BF16)
            for n in range(3):
                dabe[6 * n + u, rows] = sums[n].astype(BF16)

    dpacked = jnp.concatenate([dabe[n] for n in range(18)], axis=1)
    for half in range(2):
        lanes = slice(half * HALF, half * HALF + HALF)
        back = dot(dpacked, weight[half], NN)
        blocks = jnp.concatenate(
            [
                (cot[c, :, lanes].astype(F32) + back[128 * c : 128 * c + 128]).reshape(16, 8, HALF)
                for c in range(2)
            ],
            axis=1,
        ).astype(BF16)
        for n in range(CHIPS):
            dz_send[2 * n + half] = blocks[n]
    dz_rest = exchange(dz_send, dz_recv, 3)

    for u in range(6):
        lanes = slice(128 * u, 128 * u + 128)
        out4[:, :, lanes] = jnp.concatenate(
            [outh[c, :, lanes].astype(F32).reshape(64, 2, 128) for c in range(2)], axis=1
        ).astype(BF16)
    out_copy = pltpu.make_async_copy(out4, out, local_sem.at[6])
    out_copy.start()
    for copy in swaps:
        copy.wait_send()
    for way, steps in enumerate((up_steps, down_steps)):
        for step in range(steps):
            for part in range(2):
                ring_copy(way, step, part).wait_send()
            side_copy(way, step + 1).wait_send()
    for rest in (s_all, p_rest, z_rest):
        rest.wait_send()
    dz_rest.wait_recv()

    for t in range(PAIRS):
        lanes = slice(128 * t, 128 * t + 128)
        blocks = dz_recv[...].reshape(CHIPS, 2, 16, HALF)[:, :, :, lanes].astype(F32)
        x02, x13 = zip(*[swap2(blocks[:, c, :8], blocks[:, c, 8:]) for c in range(2)])
        r0, r2 = swap4(*x02)
        r1, r3 = swap4(*x13)
        dz = jnp.concatenate(
            [x.reshape(128, 128).astype(BF16) for x in (r0, r1, r2, r3)], axis=1
        )
        dz_rows[t] = dz
        terms(dz, wide(vh, t), g_send, t)
    g_rest = scatter(g_send, g_recv, 4)

    def store(ref, t, x):
        for r in range(4):
            ref[r, :, 128 * t : 128 * t + 128] = x[:, 128 * r : 128 * r + 128].astype(BF16)

    def give_back(ref, out_ref, n):
        local = pltpu.make_async_copy(ref.at[own_rows], out_ref.at[:, :, mine], local_sem.at[7 + n])
        away = remote(
            ref.at[their_rows], out_ref.at[:, :, mine], back_send.at[n], back_recv.at[n], sibling
        )
        landing = remote(
            ref.at[their_rows], out_ref.at[:, :, theirs], back_send.at[n], back_recv.at[n], sibling
        )
        local.start()
        away.start()
        return local, away, landing

    for t in range(PAIRS):
        dz = dz_rows[t]
        store(gvh, t, dot(gathered(p_all, 2 * t), dz * low4, TN)
              + dot(gathered(p_all, 2 * t + 1), dz * high4, TN))
    returned = [give_back(gvh, gv_out, 0)]

    dz_rest.wait_send()
    g_rest.wait_recv()
    slope = jnp.sum(g_recv[...], axis=0)
    probs = p_own[...]
    mean = jnp.sum(probs * slope, axis=-1, keepdims=True)
    ds_all[chip] = (probs * (slope - mean) * scale).astype(BF16)
    ds_rest = gather(ds_all, 5)
    out_copy.wait()
    g_rest.wait_send()
    ds_rest.wait_recv()
    for t in range(PAIRS):
        keys = wide(kh, t)
        store(gqh, t, dot(gathered(ds_all, 2 * t), keys * low4, NN)
              + dot(gathered(ds_all, 2 * t + 1), keys * high4, NN))
    returned.append(give_back(gqh, gq_out, 1))
    for t in range(PAIRS):
        query = wide(qh, t)
        store(gkh, t, dot(gathered(ds_all, 2 * t), query * low4, TN)
              + dot(gathered(ds_all, 2 * t + 1), query * high4, TN))
    returned.append(give_back(gkh, gk_out, 2))

    ds_rest.wait_send()
    for local, away, landing in returned:
        local.wait()
        away.wait_send()
        landing.wait_recv()


def on_device(planes, row_query, row_key, row_value, column_weight, cotangent):
    own_rows, columns, width = row_query.shape
    share = column_weight.shape[1]
    rows, own_columns, _ = cotangent.shape
    vmem = pltpu.VMEM
    sem = pltpu.SemaphoreType.DMA
    row_shape = jax.ShapeDtypeStruct((own_rows, columns, width), BF16)
    shapes = (jax.ShapeDtypeStruct(cotangent.shape, BF16), row_shape, row_shape, row_shape)
    results = pl.pallas_call(
        functools.partial(kernel, planes),
        out_shape=shapes,
        in_specs=[pl.BlockSpec(memory_space=pl.ANY)] * 5,
        out_specs=[pl.BlockSpec(memory_space=pl.ANY)] * 4,
        scratch_shapes=[
            vmem((4, 128, HALF), BF16),
            vmem((4, 128, HALF), BF16),
            vmem((4, 128, HALF), BF16),
            vmem((rows, own_columns, width), BF16),
            vmem((2, 128, 768), BF16),
            vmem((2, planes * share, HALF), BF16),
            vmem((128, 128), F32),
            vmem((CHIPS, 3, 16, 128), F32),
            vmem((CHIPS, 3, 16, 128), F32),
            vmem((3, 16, 128), F32),
            vmem((CHIPS, 3, 16, 128), BF16),
            vmem((2 * CHIPS, 16, HALF), BF16),
            vmem((2 * CHIPS, 16, HALF), BF16),
            vmem((256, 768), BF16),
            vmem((18, 256, 128), BF16),
            vmem((18, 256, 128), BF16),
            vmem((2, 128, 768), BF16),
            vmem((rows, own_columns, width), BF16),
            vmem((2 * CHIPS, 16, HALF), BF16),
            vmem((2 * CHIPS, 16, HALF), BF16),
            vmem((PAIRS, 128, 512), BF16),
            vmem((CHIPS, 3, 16, 128), F32),
            vmem((CHIPS, 3, 16, 128), F32),
            vmem((CHIPS, 3, 16, 128), BF16),
            vmem((4, 128, HALF), BF16),
            vmem((4, 128, HALF), BF16),
            vmem((4, 128, HALF), BF16),
            sem((10,)),
            sem((3,)), sem((3,)),
            sem((2, planes, 2)), sem((2, planes, 2)),
            sem((2, planes)), sem((2, planes)),
            sem((6,)), sem((6,)),
            sem((3,)), sem((3,)),
        ],
        compiler_params=pltpu.CompilerParams(
            collective_id=0, has_side_effects=True, vmem_limit_bytes=VMEM_LIMIT
        ),
    )(row_query, row_key, row_value, column_weight.T, cotangent)
    return pl.pallas_call(
        copy_out,
        out_shape=shapes,
        in_specs=[pl.BlockSpec(memory_space=pl.ANY)] * 4,
        out_specs=[pl.BlockSpec(memory_space=pl.ANY)] * 4,
        scratch_shapes=[sem((4,))],
        compiler_params=pltpu.CompilerParams(vmem_limit_bytes=VMEM_LIMIT),
    )(*results)


def solution(mesh):
    planes = mesh.shape["grp"]
    in_specs = (
        P(("grp", "seq"), None, None),
        P(("grp", "seq"), None, None),
        P(("grp", "seq"), None, None),
        P(None, "grp"),
        P("grp", "seq", None),
    )
    out_specs = (
        P("grp", "seq", None),
        P(("grp", "seq"), None, None),
        P(("grp", "seq"), None, None),
        P(("grp", "seq"), None, None),
    )
    return jax.shard_map(
        functools.partial(on_device, planes),
        mesh=mesh, in_specs=in_specs, out_specs=out_specs, check_vma=False,
    )
```

time: 95.7 us -> 133 us (1.39)
  Pallas kernels: 88.6 us -> 132 us
  local copies, waits for them, and re-layouts: 6.21 us -> 0 us
    pallas_call x1 -> x2, Pallas kernels: 88.6 us -> 132 us  [the longest x1 83.4 us: on_device(): pl.pallas_call(functools.partial(kernel, planes), out_shape=shapes, in_sp...]
    unnamed x11 -> x0, local copies, waits for them, and re-layouts: 4.21 us -> none
    reshape x2 -> x0, local copies, waits for them, and re-layouts: 2 us -> none  [the longest x1 1.16 us: on_device(): cotangent.reshape(rows * own_columns, width)]
where the time goes in v3:
time: 133 us
  Pallas kernels  132 us (99%)
    pallas_call x1, Pallas kernels, on_device(): pl.pallas_call(functools.partial(kernel, planes), out_shape=shapes, in_sp...  83.4 us
    pallas_call x1, Pallas kernels, on_device(): pl.pallas_call(copy_out, out_shape=shapes, in_specs=[pl.BlockSpec(memory_...  48.8 us

profile of v3, /device:TPU:1, one launch (start us, length us, event | category | flops | bytes accessed | tf_op | source)
XLA Modules:
  0.0 132.8 jit_solution(8023935029560988691)
XLA Ops:
  0.6 83.4 %shard_map.84 = (bf16[64,4,768]{2,1,0:T(4,128)(2,1)}, bf16[2,128,768]{2,1,0:T(8,128)(2,1)}, bf16[2,128,768]{2,1,0:T(8,128)(2,1)}, bf16[2,128,768]{2,1,0:T(8,128)(2,1)}) custom-call(bf16[2,128,768]{2,1,0:T(8,128)(2,1)} %q_in.1, bf16[2,128,768]{2,1,0:T(8,128)(2,1)} %k_in.1, bf16[2,128,768]{2,1,0:T(8,128)(2,1)} %v_in.1, bf16[144,768]{1,0:T(8,128)(2,1)} %bitcast.1, ...), custom_call_target="tpu_custom_call" | custom-call | tf_op jit(solution)/shard_map/pallas_call | solution.py:415
  84.0 48.8 %shard_map.85 = (bf16[64,4,768]{2,1,0:T(4,128)(2,1)}, bf16[2,128,768]{2,1,0:T(8,128)(2,1)}, bf16[2,128,768]{2,1,0:T(8,128)(2,1)}, bf16[2,128,768]{2,1,0:T(8,128)(2,1)}) custom-call(bf16[64,4,768]{2,1,0:T(4,128)(2,1)} %get-tuple-element.8.refs_0_, bf16[2,128,768]{2,1,0:T(8,128)(2,1)} %get-tuple-element.9.refs_1_, ...), custom_call_target="tpu_custom_call" | custom-call | tf_op jit(solution)/shard_map/pallas_call | solution.py:459

commit v4 on v3

--- a/solution.py
+++ b/solution.py
@@ -29,12 +29,23 @@
 
 
 def copy_out(*refs):
-    sources, targets, sem = refs[:4], refs[4:8], refs[8]
-    copies = [pltpu.make_async_copy(sources[n], targets[n], sem.at[n]) for n in range(4)]
-    for copy in copies:
-        copy.start()
-    for copy in copies:
-        copy.wait()
+    sources, targets, held, in_sem, out_sem = refs[:4], refs[4:8], refs[8:12], refs[12], refs[13]
+    pieces = []
+    for n in range(4):
+        half = sources[n].shape[0] // 2
+        for m in range(2):
+            rows = pl.ds(m * half, half)
+            pieces.append((
+                pltpu.make_async_copy(sources[n].at[rows], held[n].at[rows], in_sem.at[2 * n + m]),
+                pltpu.make_async_copy(held[n].at[rows], targets[n].at[rows], out_sem.at[2 * n + m]),
+            ))
+    for arrive, _ in pieces:
+        arrive.start()
+    for arrive, leave in pieces:
+        arrive.wait()
+        leave.start()
+    for _, leave in pieces:
+        leave.wait()
 
 
 def kernel(
@@ -54,15 +65,20 @@
     other = 1 - core
     chip_x, chip_y = lax.rem(chip, SIDE), lax.div(chip, SIDE)
     sibling = (grp, chip * 2 + other)
-    above = lax.rem(grp + 1, planes)
-    below = lax.rem(grp + planes - 1, planes)
-    up_steps = planes // 2
-    down_steps = (planes - 1) // 2
+    far = planes // 2
+    reach = (far, planes - 1 - far)
+
+    def plane(step):
+        return lax.rem(grp + planes + step, planes)
+
     scale = 1.0 / (math.sqrt(HEAD_DIM) * math.sqrt(4 * CHIPS))
 
-    targets = [None] + [
+    def hops(k):
+        return min(k % SIDE, SIDE - k % SIDE) + min(k // SIDE, SIDE - k // SIDE)
+
+    targets = [
         lax.rem(chip_y + k // SIDE, SIDE) * SIDE + lax.rem(chip_x + k % SIDE, SIDE)
-        for k in range(1, CHIPS)
+        for k in sorted(range(1, CHIPS), key=lambda k: -hops(k))
     ]
 
     def remote(src, dst, send, recv, device):
@@ -79,12 +95,10 @@
             barrier, inc=1, device_id=(grp, lax.rem(me + k, 2 * CHIPS)), device_id_type=MESH
         )
 
-    greeted = 2 * CHIPS - 1
-    if up_steps:
-        pl.semaphore_signal(barrier, inc=1, device_id=(above, me), device_id_type=MESH)
-        pl.semaphore_signal(barrier, inc=1, device_id=(below, me), device_id_type=MESH)
-        greeted += 2
-    pl.semaphore_wait(barrier, greeted)
+    near = (-2, -1, 1, 2)
+    for step in near:
+        pl.semaphore_signal(barrier, inc=1, device_id=(plane(step), me), device_id_type=MESH)
+    pl.semaphore_wait(barrier, 2 * CHIPS - 1 + len(near))
 
     mine = pl.ds(pl.multiple_of(core * HALF, HALF), HALF)
     theirs = pl.ds(pl.multiple_of(other * HALF, HALF), HALF)
@@ -103,35 +117,54 @@
         locals_[n].start()
 
     share = w_in.shape[0]
-    first = (share // 16 + 1) // 2 * 16
-    cuts = ((0, first), (first, share - first))
-
-    def block_rows(way, step):
-        block = lax.rem(grp + planes - step, planes) if way == 0 else lax.rem(grp + step, planes)
-        return pl.multiple_of(block * share, 16)
-
-    def ring_copy(way, step, part):
-        begin, size = cuts[part]
-        rows = pl.ds(pl.multiple_of(block_rows(way, step) + begin, 16), size)
-        src = w_in.at[pl.ds(begin, size), mine] if step == 0 else weight.at[core, rows]
+
+    def block_rows(way, distance):
+        return pl.ds(pl.multiple_of(plane(distance if way else -distance) * share, 16), share)
+
+    def ring_copy(way, distance):
+        jump = 2 - distance % 2
+        begin = distance - jump
+        rows = block_rows(way, begin)
+        src = w_in.at[:, mine] if begin == 0 else weight.at[core, rows]
         return remote(
-            src, weight.at[core, rows], ring_send.at[way, step, part],
-            ring_recv.at[way, step, part], (below if way else above, me),
-        )
-
-    def side_copy(way, step):
-        rows = weight.at[core, pl.ds(block_rows(way, step), share)]
-        return remote(rows, rows, side_send.at[way, step], side_recv.at[way, step], sibling)
-
-    for part in range(2):
-        if up_steps:
-            ring_copy(0, 0, part).start()
-        if down_steps:
-            ring_copy(1, 0, part).start()
+            src, weight.at[core, rows], ring_send.at[way, distance],
+            ring_recv.at[way, distance], (plane(-jump if way else jump), me),
+        )
+
+    def side_copy(way, distance):
+        rows = weight.at[core, block_rows(way, distance)]
+        return remote(
+            rows, rows, side_send.at[way, distance], side_recv.at[way, distance], sibling
+        )
+
+    def ring_start(begin):
+        for way in range(2):
+            for distance in (begin + 2, begin + 1):
+                if distance <= reach[way]:
+                    ring_copy(way, distance).start()
+
+    def ring_arrive(distance):
+        for way in range(2):
+            if distance <= reach[way]:
+                ring_copy(way, distance).wait_recv()
+
+    def side_start(distance):
+        for way in range(2):
+            if distance <= reach[way]:
+                side_copy(way, distance).start()
+
+    def ring(begin):
+        ring_arrive(begin)
+        ring_start(begin)
+        side_start(begin)
+        ring_arrive(begin - 1)
+        side_start(begin - 1)
+
+    ring_start(0)
     weight_own = [
         pltpu.make_async_copy(
             w_in.at[:, pl.ds(half * HALF, HALF)],
-            weight.at[half, pl.ds(block_rows(0, 0), share)], local_sem.at[3 + half],
+            weight.at[half, block_rows(0, 0)], local_sem.at[3 + half],
         )
         for half in range(2)
     ]
@@ -140,25 +173,14 @@
     cot_copy = pltpu.make_async_copy(cot_in, cot4, local_sem.at[5])
     cot_copy.start()
 
-    def ring(first_turn, last_turn):
-        for turn in range(first_turn, last_turn):
-            step, part = turn // 2 + 1, turn % 2
-            for way, steps in enumerate((up_steps, down_steps)):
-                if step <= steps:
-                    ring_copy(way, step - 1, part).wait_recv()
-                    if step < steps:
-                        ring_copy(way, step, part).start()
-                    if part == 1:
-                        side_copy(way, step).start()
-
     lane = lax.broadcasted_iota(jnp.int32, (1, 128), 1)
     low = jnp.where(lane < HEAD_DIM, 1.0, 0.0).astype(BF16)
     high = jnp.where(lane < HEAD_DIM, 0.0, 1.0).astype(BF16)
     low4 = jnp.concatenate([low] * 4, axis=1)
     high4 = jnp.concatenate([high] * 4, axis=1)
-    row_id = lax.broadcasted_iota(jnp.int32, (128, 128), 0)
-    col_id = lax.broadcasted_iota(jnp.int32, (128, 128), 1)
-    bias[...] = jnp.where(row_id % 2 == col_id % 2, 0.0, -1e30)
+    row_id = lax.broadcasted_iota(jnp.int32, (128, 256), 0)
+    col_id = lax.broadcasted_iota(jnp.int32, (128, 256), 1)
+    bias[...] = jnp.where(lax.rem(row_id, 2) == lax.rem(col_id, 2), 0.0, -1e30)
 
     def wide(ref, t):
         return jnp.concatenate([ref[r, :, 128 * t : 128 * t + 128] for r in range(4)], axis=1)
@@ -173,8 +195,7 @@
         return ref[8 * (h // 3) : 8 * (h // 3) + 8, h % 3].reshape(128, 128)
 
     def scatter(send_ref, recv_ref, n):
-        for k in range(1, CHIPS):
-            to = targets[k]
+        for to in targets:
             remote(
                 send_ref.at[to], recv_ref.at[chip], many_send.at[n], many_recv.at[n],
                 (grp, to * 2 + core),
@@ -186,17 +207,17 @@
         )
 
     def gather(ref, n):
-        for k in range(1, CHIPS):
+        for to in targets:
             remote(
                 ref.at[chip], ref.at[chip], many_send.at[n], many_recv.at[n],
-                (grp, targets[k] * 2 + core),
+                (grp, to * 2 + core),
             ).start()
         rest = pl.ds(0, CHIPS - 1)
         return remote(ref.at[rest], ref.at[rest], many_send.at[n], many_recv.at[n], sibling)
 
     def exchange(send_ref, recv_ref, n):
-        for k in range(1, CHIPS):
-            for to in (targets[k] * 2 + core, targets[k] * 2 + other):
+        for partner in targets:
+            for to in (partner * 2 + core, partner * 2 + other):
                 remote(
                     send_ref.at[to], recv_ref.at[me], many_send.at[n], many_recv.at[n], (grp, to)
                 ).start()
@@ -226,7 +247,7 @@
     for t in range(PAIRS):
         terms(wide(qh, t), wide(kh, t), s_send, t)
     s_all = scatter(s_send, s_recv, 0)
-    ring(0, 3)
+    ring(2)
     s_all.wait_recv()
     scores = jnp.sum(s_recv[...], axis=0) * scale
     shifted = jnp.exp(scores - jnp.max(scores, axis=-1, keepdims=True))
@@ -234,13 +255,13 @@
     p_own[...] = probs
     p_all[chip] = probs.astype(BF16)
     p_rest = gather(p_all, 1)
-    ring(3, 6)
     cot_copy.wait()
     for u in range(6):
         lanes = slice(128 * u, 128 * u + 128)
         g4 = cot4[:, :, lanes].astype(F32)
         for c in range(2):
             cot[c, :, lanes] = g4[:, 2 * c : 2 * c + 2].reshape(128, 128).astype(BF16)
+    ring(4)
     swaps[2].wait_recv()
     locals_[2].wait()
     p_rest.wait_recv()
@@ -257,14 +278,14 @@
             for n in range(CHIPS):
                 z_send[2 * n + c, :, lanes] = block[n]
     z_rest = exchange(z_send, z_recv, 2)
-    ring(6, 2 * up_steps)
+    for begin in range(6, far + 1, 2):
+        ring(begin)
 
     for copy in weight_own:
         copy.wait()
-    for step in range(1, up_steps + 1):
-        side_copy(0, step).wait_recv()
-    for step in range(1, down_steps + 1):
-        side_copy(1, step).wait_recv()
+    for way in range(2):
+        for distance in range(1, reach[way] + 1):
+            side_copy(way, distance).wait_recv()
     z_rest.wait_recv()
 
     arrived = z_recv[...].reshape(CHIPS, 2, 16, HALF)
@@ -286,27 +307,28 @@
     @pl.loop(0, 6)
     def _(u):
         lanes = pl.ds(pl.multiple_of(u * 128, 128), 128)
-        for c in range(2):
-            rows = slice(128 * c, 128 * c + 128)
-            a, b, e = abe[u, rows], abe[6 + u, rows], abe[12 + u, rows]
-            g = cot[c, :, lanes]
-            att = zh[rows, lanes].astype(F32)
-            sums = None
-            for keep in (low, high):
-                ak, bk, ek, gk = a * keep, b * keep, e * keep, g * keep
-                logits = dot(a, bk, NT) * 0.125 + bias[...]
-                shifted = jnp.exp(logits - jnp.max(logits, axis=-1, keepdims=True))
-                weights = shifted * (1.0 / jnp.sum(shifted, axis=-1, keepdims=True))
-                weights_low = weights.astype(BF16)
-                slope = dot(g, ek, NT)
-                mean = jnp.sum(weights * slope, axis=-1, keepdims=True)
-                dlogits = (weights * (slope - mean) * 0.125).astype(BF16)
-                att = att + dot(weights_low, ek, NN)
-                parts = (dot(dlogits, bk, NN), dot(dlogits, ak, TN), dot(weights_low, gk, TN))
-                sums = parts if sums is None else [x + y for x, y in zip(sums, parts)]
+        both = range(2)
+        rows = [slice(128 * c, 128 * c + 128) for c in both]
+        split = lambda x: jnp.concatenate([x * low, x * high], axis=0)
+        stack = lambda x: jnp.concatenate([x[:, :128], x[:, 128:]], axis=0)
+        a, b, e = ([abe[6 * n + u, rows[c]] for c in both] for n in range(3))
+        g = [cot[c, :, lanes] for c in both]
+        a2, b2, e2, g2 = ([split(x) for x in xs] for xs in (a, b, e, g))
+        logits = [dot(b[c], a2[c], NT) * 0.125 + bias[...] for c in both]
+        slope = [dot(e[c], g2[c], NT) for c in both]
+        shifted = [jnp.exp(x - jnp.max(x, axis=0, keepdims=True)) for x in logits]
+        weights = [x * (1.0 / jnp.sum(x, axis=0, keepdims=True)) for x in shifted]
+        weights_low = [x.astype(BF16) for x in weights]
+        mean = [jnp.sum(x * y, axis=0, keepdims=True) for x, y in zip(weights, slope)]
+        dlogits = [
+            (weights[c] * (slope[c] - mean[c]) * 0.125).astype(BF16) for c in both
+        ]
+        for c in both:
+            att = zh[rows[c], lanes].astype(F32) + dot(stack(weights_low[c]), e2[c], TN)
             outh[c, :, lanes] = att.astype(BF16)
-            for n in range(3):
-                dabe[6 * n + u, rows] = sums[n].astype(BF16)
+            dabe[12 + u, rows[c]] = dot(weights_low[c], g2[c], NN).astype(BF16)
+            dabe[u, rows[c]] = dot(stack(dlogits[c]), b2[c], TN).astype(BF16)
+            dabe[6 + u, rows[c]] = dot(dlogits[c], a2[c], NN).astype(BF16)
 
     dpacked = jnp.concatenate([dabe[n] for n in range(18)], axis=1)
     for half in range(2):
@@ -332,11 +354,10 @@
     out_copy.start()
     for copy in swaps:
         copy.wait_send()
-    for way, steps in enumerate((up_steps, down_steps)):
-        for step in range(steps):
-            for part in range(2):
-                ring_copy(way, step, part).wait_send()
-            side_copy(way, step + 1).wait_send()
+    for way in range(2):
+        for distance in range(1, reach[way] + 1):
+            ring_copy(way, distance).wait_send()
+            side_copy(way, distance).wait_send()
     for rest in (s_all, p_rest, z_rest):
         rest.wait_send()
     dz_rest.wait_recv()
@@ -424,7 +445,7 @@
             vmem((rows, own_columns, width), BF16),
             vmem((2, 128, 768), BF16),
             vmem((2, planes * share, HALF), BF16),
-            vmem((128, 128), F32),
+            vmem((128, 256), F32),
             vmem((CHIPS, 3, 16, 128), F32),
             vmem((CHIPS, 3, 16, 128), F32),
             vmem((3, 16, 128), F32),
@@ -447,7 +468,7 @@
             vmem((4, 128, HALF), BF16),
             sem((10,)),
             sem((3,)), sem((3,)),
-            sem((2, planes, 2)), sem((2, planes, 2)),
+            sem((2, planes)), sem((2, planes)),
             sem((2, planes)), sem((2, planes)),
             sem((6,)), sem((6,)),
             sem((3,)), sem((3,)),
@@ -461,7 +482,7 @@
         out_shape=shapes,
         in_specs=[pl.BlockSpec(memory_space=pl.ANY)] * 4,
         out_specs=[pl.BlockSpec(memory_space=pl.ANY)] * 4,
-        scratch_shapes=[sem((4,))],
+        scratch_shapes=[vmem(x.shape, BF16) for x in shapes] + [sem((8,)), sem((8,))],
         compiler_params=pltpu.CompilerParams(vmem_limit_bytes=VMEM_LIMIT),
     )(*results)
 

time: 133 us -> 79.5 us (0.60)
  Pallas kernels: 132 us -> 78.7 us
    pallas_call x1, Pallas kernels: 48.8 us -> 2.29 us  [on_device(): pl.pallas_call(copy_out, out_shape=shapes, in_specs=[pl.BlockSpec(memory_...]
    pallas_call x1, Pallas kernels: 83.4 us -> 76.4 us  [on_device(): pl.pallas_call(functools.partial(kernel, planes), out_shape=shapes, in_sp...]
where the time goes in v4:
time: 79.5 us; the launch traced here: 79.3 us
  Pallas kernels  78.7 us (99%)
    pallas_call x1, Pallas kernels, on_device(): pl.pallas_call(functools.partial(kernel, planes), out_shape=shapes, in_sp...  76.4 us
    pallas_call x1, Pallas kernels, on_device(): pl.pallas_call(copy_out, out_shape=shapes, in_specs=[pl.BlockSpec(memory_...  2.29 us

profile of v4, /device:TPU:1, one launch (start us, length us, event | category | flops | bytes accessed | tf_op | source)
XLA Modules:
  0.0 79.3 jit_solution(207392083792745031)
XLA Ops:
  0.6 76.4 %shard_map.84 = (bf16[64,4,768]{2,1,0:T(4,128)(2,1)}, bf16[2,128,768]{2,1,0:T(8,128)(2,1)}, bf16[2,128,768]{2,1,0:T(8,128)(2,1)}, bf16[2,128,768]{2,1,0:T(8,128)(2,1)}) custom-call(bf16[2,128,768]{2,1,0:T(8,128)(2,1)} %q_in.1, bf16[2,128,768]{2,1,0:T(8,128)(2,1)} %k_in.1, bf16[2,128,768]{2,1,0:T(8,128)(2,1)} %v_in.1, bf16[144,768]{1,0:T(8,128)(2,1)} %bitcast.1, ...), custom_call_target="tpu_custom_call" | custom-call | tf_op jit(solution)/shard_map/pallas_call | solution.py:436
  77.0 2.3 %shard_map.85 = (bf16[64,4,768]{2,1,0:T(4,128)(2,1)}, bf16[2,128,768]{2,1,0:T(8,128)(2,1)}, bf16[2,128,768]{2,1,0:T(8,128)(2,1)}, bf16[2,128,768]{2,1,0:T(8,128)(2,1)}) custom-call(bf16[64,4,768]{2,1,0:T(4,128)(2,1)} %get-tuple-element.8.refs_0_, bf16[2,128,768]{2,1,0:T(8,128)(2,1)} %get-tuple-element.9.refs_1_, ...), custom_call_target="tpu_custom_call" | custom-call | tf_op jit(solution)/shard_map/pallas_call | solution.py:480

commit v5 on v4

--- a/solution.py
+++ b/solution.py
@@ -55,7 +55,8 @@
     qh, kh, vh, cot4, cot, weight, bias,
     s_send, s_recv, p_own, p_all, z_send, z_recv, zh, abe, dabe, outh, out4,
     dz_send, dz_recv, dz_rows, g_send, g_recv, ds_all, gqh, gkh, gvh,
-    local_sem, swap_send, swap_recv, ring_send, ring_recv, side_send, side_recv,
+    local_sem, swap_send, swap_recv, ring_send, ring_recv, mate_send, mate_recv,
+    side_send, side_recv,
     many_send, many_recv, back_send, back_recv,
 ):
     grp = lax.axis_index("grp")
@@ -117,24 +118,53 @@
         locals_[n].start()
 
     share = w_in.shape[0]
-
-    def block_rows(way, distance):
-        return pl.ds(pl.multiple_of(plane(distance if way else -distance) * share, 16), share)
+    lead = (share // 16 + 1) // 2 * 16
+    tail = share - lead
+    parity = (lax.rem(chip_x, 2), lax.rem(chip_y, 2))
+    mate = (
+        (grp, (chip + 1 - 2 * parity[0]) * 2 + core),
+        (grp, (chip + SIDE - 2 * SIDE * parity[1]) * 2 + core),
+    )
+
+    def block_begin(way, distance):
+        return plane(distance if way else -distance) * share
+
+    def part_rows(way, distance, part):
+        begin = (parity[way] * tail, parity[way] * lead, (1 - parity[way]) * lead)[part]
+        size = (lead, tail, tail)[part]
+        return pl.ds(pl.multiple_of(block_begin(way, distance) + begin, 16), size)
 
     def ring_copy(way, distance):
         jump = 2 - distance % 2
         begin = distance - jump
-        rows = block_rows(way, begin)
-        src = w_in.at[:, mine] if begin == 0 else weight.at[core, rows]
+        rows = part_rows(way, begin, 0)
+        if begin == 0:
+            src = w_in.at[pl.ds(pl.multiple_of(parity[way] * tail, 16), lead), mine]
+        else:
+            src = weight.at[core, rows]
         return remote(
             src, weight.at[core, rows], ring_send.at[way, distance],
             ring_recv.at[way, distance], (plane(-jump if way else jump), me),
         )
 
-    def side_copy(way, distance):
-        rows = weight.at[core, block_rows(way, distance)]
+    def mate_copy(way, distance):
+        rows = weight.at[core, part_rows(way, distance, 1)]
+        return remote(rows, rows, mate_send.at[way, distance], mate_recv.at[way, distance], mate[way])
+
+    def mate_landing(way, distance):
+        rows = weight.at[core, part_rows(way, distance, 2)]
+        return remote(rows, rows, mate_send.at[way, distance], mate_recv.at[way, distance], mate[way])
+
+    def side_copy(way, distance, part):
+        rows = weight.at[core, part_rows(way, distance, 2 * part)]
         return remote(
-            rows, rows, side_send.at[way, distance], side_recv.at[way, distance], sibling
+            rows, rows, side_send.at[way, distance, part], side_recv.at[way, distance, part], sibling
+        )
+
+    def side_landing(way, distance, part):
+        rows = weight.at[other, part_rows(way, distance, 2 * part)]
+        return remote(
+            rows, rows, side_send.at[way, distance, part], side_recv.at[way, distance, part], sibling
         )
 
     def ring_start(begin):
@@ -148,23 +178,31 @@
             if distance <= reach[way]:
                 ring_copy(way, distance).wait_recv()
 
-    def side_start(distance):
+    def share_start(distance):
         for way in range(2):
             if distance <= reach[way]:
-                side_copy(way, distance).start()
+                mate_copy(way, distance).start()
+                side_copy(way, distance, 0).start()
 
     def ring(begin):
         ring_arrive(begin)
         ring_start(begin)
-        side_start(begin)
+        share_start(begin)
         ring_arrive(begin - 1)
-        side_start(begin - 1)
+        share_start(begin - 1)
+
+    def mated(begin):
+        for distance in (begin, begin - 1):
+            for way in range(2):
+                if distance <= reach[way]:
+                    mate_landing(way, distance).wait_recv()
+                    side_copy(way, distance, 1).start()
 
     ring_start(0)
     weight_own = [
         pltpu.make_async_copy(
             w_in.at[:, pl.ds(half * HALF, HALF)],
-            weight.at[half, block_rows(0, 0)], local_sem.at[3 + half],
+            weight.at[half, pl.ds(pl.multiple_of(block_begin(0, 0), 16), share)], local_sem.at[3 + half],
         )
         for half in range(2)
     ]
@@ -262,6 +300,7 @@
         for c in range(2):
             cot[c, :, lanes] = g4[:, 2 * c : 2 * c + 2].reshape(128, 128).astype(BF16)
     ring(4)
+    mated(2)
     swaps[2].wait_recv()
     locals_[2].wait()
     p_rest.wait_recv()
@@ -280,12 +319,15 @@
     z_rest = exchange(z_send, z_recv, 2)
     for begin in range(6, far + 1, 2):
         ring(begin)
+        mated(begin - 2)
+    mated(far)
 
     for copy in weight_own:
         copy.wait()
     for way in range(2):
         for distance in range(1, reach[way] + 1):
-            side_copy(way, distance).wait_recv()
+            for part in range(2):
+                side_landing(way, distance, part).wait_recv()
     z_rest.wait_recv()
 
     arrived = z_recv[...].reshape(CHIPS, 2, 16, HALF)
@@ -357,7 +399,9 @@
     for way in range(2):
         for distance in range(1, reach[way] + 1):
             ring_copy(way, distance).wait_send()
-            side_copy(way, distance).wait_send()
+            mate_copy(way, distance).wait_send()
+            for part in range(2):
+                side_copy(way, distance, part).wait_send()
     for rest in (s_all, p_rest, z_rest):
         rest.wait_send()
     dz_rest.wait_recv()
@@ -470,6 +514,7 @@
             sem((3,)), sem((3,)),
             sem((2, planes)), sem((2, planes)),
             sem((2, planes)), sem((2, planes)),
+            sem((2, planes, 2)), sem((2, planes, 2)),
             sem((6,)), sem((6,)),
             sem((3,)), sem((3,)),
         ],

time: 79.5 us -> 73.5 us (0.925)
  Pallas kernels: 78.7 us -> 72.7 us
    pallas_call x1, Pallas kernels: 76.4 us -> 70.4 us  [on_device(): pl.pallas_call(functools.partial(kernel, planes), out_shape=shapes, in_sp...]
where the time goes in v5:
time: 73.5 us; the launch traced here: 73.3 us
  Pallas kernels  72.7 us (99%)
    pallas_call x1, Pallas kernels, on_device(): pl.pallas_call(functools.partial(kernel, planes), out_shape=shapes, in_sp...  70.4 us
    pallas_call x1, Pallas kernels, on_device(): pl.pallas_call(copy_out, out_shape=shapes, in_specs=[pl.BlockSpec(memory_...  2.29 us

profile of v5, /device:TPU:1, one launch (start us, length us, event | category | flops | bytes accessed | tf_op | source)
XLA Modules:
  0.0 73.3 jit_solution(11749263601602399610)
XLA Ops:
  0.6 70.4 %shard_map.84 = (bf16[64,4,768]{2,1,0:T(4,128)(2,1)}, bf16[2,128,768]{2,1,0:T(8,128)(2,1)}, bf16[2,128,768]{2,1,0:T(8,128)(2,1)}, bf16[2,128,768]{2,1,0:T(8,128)(2,1)}) custom-call(bf16[2,128,768]{2,1,0:T(8,128)(2,1)} %q_in.1, bf16[2,128,768]{2,1,0:T(8,128)(2,1)} %k_in.1, bf16[2,128,768]{2,1,0:T(8,128)(2,1)} %v_in.1, bf16[144,768]{1,0:T(8,128)(2,1)} %bitcast.1, ...), custom_call_target="tpu_custom_call" | custom-call | tf_op jit(solution)/shard_map/pallas_call | solution.py:480
  71.0 2.3 %shard_map.85 = (bf16[64,4,768]{2,1,0:T(4,128)(2,1)}, bf16[2,128,768]{2,1,0:T(8,128)(2,1)}, bf16[2,128,768]{2,1,0:T(8,128)(2,1)}, bf16[2,128,768]{2,1,0:T(8,128)(2,1)}) custom-call(bf16[64,4,768]{2,1,0:T(4,128)(2,1)} %get-tuple-element.8.refs_0_, bf16[2,128,768]{2,1,0:T(8,128)(2,1)} %get-tuple-element.9.refs_1_, ...), custom_call_target="tpu_custom_call" | custom-call | tf_op jit(solution)/shard_map/pallas_call | solution.py:525

commit v6 on v5

--- a/solution.py
+++ b/solution.py
@@ -13,6 +13,7 @@
 CHIPS = 16
 SIDE = 4
 HALF = 384
+PIECES = 2
 PAIRS = 3
 MESH = pl.DeviceIdType.MESH
 VMEM_LIMIT = 60 * 1024 * 1024
@@ -32,12 +33,12 @@
     sources, targets, held, in_sem, out_sem = refs[:4], refs[4:8], refs[8:12], refs[12], refs[13]
     pieces = []
     for n in range(4):
-        half = sources[n].shape[0] // 2
-        for m in range(2):
-            rows = pl.ds(m * half, half)
+        for m in range(PIECES):
+            size = sources[n].shape[0] // 2
+            rows, lanes = pl.ds(m % 2 * size, size), pl.ds(0, 768)
             pieces.append((
-                pltpu.make_async_copy(sources[n].at[rows], held[n].at[rows], in_sem.at[2 * n + m]),
-                pltpu.make_async_copy(held[n].at[rows], targets[n].at[rows], out_sem.at[2 * n + m]),
+                pltpu.make_async_copy(sources[n].at[rows, :, lanes], held[n].at[rows, :, lanes], in_sem.at[PIECES * n + m]),
+                pltpu.make_async_copy(held[n].at[rows, :, lanes], targets[n].at[rows, :, lanes], out_sem.at[PIECES * n + m]),
             ))
     for arrive, _ in pieces:
         arrive.start()
@@ -89,17 +90,13 @@
         )
 
     barrier = pltpu.get_barrier_semaphore()
-
-    @pl.loop(1, 2 * CHIPS)
-    def _(k):
-        pl.semaphore_signal(
-            barrier, inc=1, device_id=(grp, lax.rem(me + k, 2 * CHIPS)), device_id_type=MESH
-        )
-
     near = (-2, -1, 1, 2)
-    for step in near:
-        pl.semaphore_signal(barrier, inc=1, device_id=(plane(step), me), device_id_type=MESH)
-    pl.semaphore_wait(barrier, 2 * CHIPS - 1 + len(near))
+    for device in (
+        [(plane(step), me) for step in near]
+        + [(grp, to * 2 + core) for to in targets]
+        + [sibling]
+    ):
+        pl.semaphore_signal(barrier, inc=1, device_id=device, device_id_type=MESH)
 
     mine = pl.ds(pl.multiple_of(core * HALF, HALF), HALF)
     theirs = pl.ds(pl.multiple_of(other * HALF, HALF), HALF)
@@ -114,7 +111,6 @@
             pltpu.make_async_copy(src.at[:, :, mine], dst.at[own_rows], local_sem.at[n])
         )
     for n in range(3):
-        swaps[n].start()
         locals_[n].start()
 
     share = w_in.shape[0]
@@ -198,7 +194,6 @@
                     mate_landing(way, distance).wait_recv()
                     side_copy(way, distance, 1).start()
 
-    ring_start(0)
     weight_own = [
         pltpu.make_async_copy(
             w_in.at[:, pl.ds(half * HALF, HALF)],
@@ -210,6 +205,12 @@
         copy.start()
     cot_copy = pltpu.make_async_copy(cot_in, cot4, local_sem.at[5])
     cot_copy.start()
+
+    pl.semaphore_wait(barrier, CHIPS + len(near))
+    ring_start(0)
+
+    for n in range(2):
+        swaps[n].start()
 
     lane = lax.broadcasted_iota(jnp.int32, (1, 128), 1)
     low = jnp.where(lane < HEAD_DIM, 1.0, 0.0).astype(BF16)
@@ -253,16 +254,13 @@
         rest = pl.ds(0, CHIPS - 1)
         return remote(ref.at[rest], ref.at[rest], many_send.at[n], many_recv.at[n], sibling)
 
-    def exchange(send_ref, recv_ref, n):
-        for partner in targets:
-            for to in (partner * 2 + core, partner * 2 + other):
-                remote(
-                    send_ref.at[to], recv_ref.at[me], many_send.at[n], many_recv.at[n], (grp, to)
-                ).start()
+    def send_block(send_ref, recv_ref, n, to):
         remote(
-            send_ref.at[chip * 2 + other], recv_ref.at[me], many_send.at[n], many_recv.at[n],
-            sibling,
+            send_ref.at[to], recv_ref.at[me], many_send.at[n], many_recv.at[n], (grp, to)
         ).start()
+
+    def exchange_end(send_ref, recv_ref, n):
+        send_block(send_ref, recv_ref, n, chip * 2 + other)
         recv_ref[me] = send_ref[me]
         rest = pl.ds(0, 2 * CHIPS - 1)
         return remote(
@@ -285,6 +283,7 @@
     for t in range(PAIRS):
         terms(wide(qh, t), wide(kh, t), s_send, t)
     s_all = scatter(s_send, s_recv, 0)
+    swaps[2].start()
     ring(2)
     s_all.wait_recv()
     scores = jnp.sum(s_recv[...], axis=0) * scale
@@ -316,7 +315,10 @@
             block = jnp.concatenate(swap2(x, y), axis=1).astype(BF16)
             for n in range(CHIPS):
                 z_send[2 * n + c, :, lanes] = block[n]
-    z_rest = exchange(z_send, z_recv, 2)
+    for to in targets:
+        send_block(z_send, z_recv, 2, to * 2 + core)
+        send_block(z_send, z_recv, 2, to * 2 + other)
+    z_rest = exchange_end(z_send, z_recv, 2)
     for begin in range(6, far + 1, 2):
         ring(begin)
         mated(begin - 2)
@@ -346,7 +348,7 @@
         for u in range(6):
             abe[6 * part + u] = packed[:, 128 * u : 128 * u + 128]
 
-    @pl.loop(0, 6)
+    @pl.loop(0, 6, unroll=6)
     def _(u):
         lanes = pl.ds(pl.multiple_of(u * 128, 128), 128)
         both = range(2)
@@ -385,7 +387,9 @@
         ).astype(BF16)
         for n in range(CHIPS):
             dz_send[2 * n + half] = blocks[n]
-    dz_rest = exchange(dz_send, dz_recv, 3)
+        for to in targets:
+            send_block(dz_send, dz_recv, 3, to * 2 + half)
+    dz_rest = exchange_end(dz_send, dz_recv, 3)
 
     for u in range(6):
         lanes = slice(128 * u, 128 * u + 128)
@@ -527,7 +531,7 @@
         out_shape=shapes,
         in_specs=[pl.BlockSpec(memory_space=pl.ANY)] * 4,
         out_specs=[pl.BlockSpec(memory_space=pl.ANY)] * 4,
-        scratch_shapes=[vmem(x.shape, BF16) for x in shapes] + [sem((8,)), sem((8,))],
+        scratch_shapes=[vmem(x.shape, BF16) for x in shapes] + [sem((4 * PIECES,))] * 2,
         compiler_params=pltpu.CompilerParams(vmem_limit_bytes=VMEM_LIMIT),
     )(*results)
 

time: 73.5 us -> 70.4 us (0.958)
  Pallas kernels: 72.7 us -> 69.6 us
    pallas_call x1, Pallas kernels: 70.4 us -> 67.4 us  [on_device(): pl.pallas_call(functools.partial(kernel, planes), out_shape=shapes, in_sp...]
where the time goes in v6:
time: 70.4 us; the launch traced here: 70.3 us
  Pallas kernels  69.6 us (99%)
    pallas_call x1, Pallas kernels, on_device(): pl.pallas_call(functools.partial(kernel, planes), out_shape=shapes, in_sp...  67.4 us
    pallas_call x1, Pallas kernels, on_device(): pl.pallas_call(copy_out, out_shape=shapes, in_specs=[pl.BlockSpec(memory_...  2.29 us

profile of v6, /device:TPU:1, one launch (start us, length us, event | category | flops | bytes accessed | tf_op | source)
XLA Modules:
  0.0 70.3 jit_solution(18000333163219198853)
XLA Ops:
  0.6 67.4 %shard_map.84 = (bf16[64,4,768]{2,1,0:T(4,128)(2,1)}, bf16[2,128,768]{2,1,0:T(8,128)(2,1)}, bf16[2,128,768]{2,1,0:T(8,128)(2,1)}, bf16[2,128,768]{2,1,0:T(8,128)(2,1)}) custom-call(bf16[2,128,768]{2,1,0:T(8,128)(2,1)} %q_in.1, bf16[2,128,768]{2,1,0:T(8,128)(2,1)} %k_in.1, bf16[2,128,768]{2,1,0:T(8,128)(2,1)} %v_in.1, bf16[144,768]{1,0:T(8,128)(2,1)} %bitcast.1, ...), custom_call_target="tpu_custom_call" | custom-call | tf_op jit(solution)/shard_map/pallas_call | solution.py:484
  68.0 2.3 %shard_map.85 = (bf16[64,4,768]{2,1,0:T(4,128)(2,1)}, bf16[2,128,768]{2,1,0:T(8,128)(2,1)}, bf16[2,128,768]{2,1,0:T(8,128)(2,1)}, bf16[2,128,768]{2,1,0:T(8,128)(2,1)}) custom-call(bf16[64,4,768]{2,1,0:T(4,128)(2,1)} %get-tuple-element.8.refs_0_, bf16[2,128,768]{2,1,0:T(8,128)(2,1)} %get-tuple-element.9.refs_1_, ...), custom_call_target="tpu_custom_call" | custom-call | tf_op jit(solution)/shard_map/pallas_call | solution.py:529

commit v7 on v6

--- a/solution.py
+++ b/solution.py
@@ -13,7 +13,6 @@
 CHIPS = 16
 SIDE = 4
 HALF = 384
-PIECES = 2
 PAIRS = 3
 MESH = pl.DeviceIdType.MESH
 VMEM_LIMIT = 60 * 1024 * 1024
@@ -29,36 +28,78 @@
     return lax.dot_general(x, y, dims, preferred_element_type=F32)
 
 
-def copy_out(*refs):
-    sources, targets, held, in_sem, out_sem = refs[:4], refs[4:8], refs[8:12], refs[12], refs[13]
-    pieces = []
-    for n in range(4):
-        for m in range(PIECES):
-            size = sources[n].shape[0] // 2
-            rows, lanes = pl.ds(m % 2 * size, size), pl.ds(0, 768)
-            pieces.append((
-                pltpu.make_async_copy(sources[n].at[rows, :, lanes], held[n].at[rows, :, lanes], in_sem.at[PIECES * n + m]),
-                pltpu.make_async_copy(held[n].at[rows, :, lanes], targets[n].at[rows, :, lanes], out_sem.at[PIECES * n + m]),
-            ))
-    for arrive, _ in pieces:
-        arrive.start()
-    for arrive, leave in pieces:
-        arrive.wait()
-        leave.start()
-    for _, leave in pieces:
-        leave.wait()
+def finish(
+    q_in, k_in, ds_in, out_in, gv_in,
+    out, gq_out, gk_out, gv_out,
+    q, k, ds, out_held, gv_held, gq, gk, in_sem, out_sem,
+):
+    low, high = head_masks(2)
+    arrive = [
+        pltpu.make_async_copy(src, dst, in_sem.at[n])
+        for n, (src, dst) in enumerate(
+            ((ds_in, ds), (k_in, k), (q_in, q), (out_in, out_held), (gv_in, gv_held))
+        )
+    ]
+    for copy in arrive:
+        copy.start()
+    leave = [
+        pltpu.make_async_copy(out_held, out, out_sem.at[0]),
+        pltpu.make_async_copy(gv_held, gv_out, out_sem.at[1]),
+    ]
+
+    def gradient(held, other, dims, target, n):
+        for t in range(2 * PAIRS):
+            lanes = slice(128 * t, 128 * t + 128)
+            x = jnp.concatenate([other[r, :, lanes] for r in range(2)], axis=1)
+            total = None
+            for e, keep in enumerate((low, high)):
+                h = 2 * t + e
+                group, place = h % 6 // 3, h % 3
+                rows = jnp.concatenate(
+                    [ds[h // 6, 8 * group + b, place] for b in range(8)], axis=0
+                )
+                part = dot(rows, x * keep, dims)
+                total = part if total is None else total + part
+            for r in range(2):
+                held[r, :, lanes] = total[:, 128 * r : 128 * r + 128].astype(BF16)
+            if t % PAIRS == PAIRS - 1:
+                half = pl.ds(t // PAIRS * HALF, HALF)
+                leave.append(
+                    pltpu.make_async_copy(
+                        held.at[:, :, half], target.at[:, :, half], out_sem.at[n + t // PAIRS]
+                    )
+                )
+                leave[-1].start()
+
+    arrive[0].wait()
+    arrive[1].wait()
+    gradient(gq, k, NN, gq_out, 2)
+    for n in range(2):
+        arrive[3 + n].wait()
+        leave[n].start()
+    arrive[2].wait()
+    gradient(gk, q, TN, gk_out, 4)
+    for copy in leave:
+        copy.wait()
+
+
+def head_masks(copies):
+    lane = lax.broadcasted_iota(jnp.int32, (1, 128), 1)
+    low = jnp.where(lane < HEAD_DIM, 1.0, 0.0).astype(BF16)
+    high = jnp.where(lane < HEAD_DIM, 0.0, 1.0).astype(BF16)
+    return [jnp.concatenate([x] * copies, axis=1) for x in (low, high)]
 
 
 def kernel(
     planes,
     q_in, k_in, v_in, w_in, cot_in,
-    out, gq_out, gk_out, gv_out,
+    out, ds_out, gv_out,
     qh, kh, vh, cot4, cot, weight, bias,
     s_send, s_recv, p_own, p_all, z_send, z_recv, zh, abe, dabe, outh, out4,
-    dz_send, dz_recv, dz_rows, g_send, g_recv, ds_all, gqh, gkh, gvh,
+    dz_send, dz_recv, dz_rows, g_send, g_recv, ds_all, gvh,
     local_sem, swap_send, swap_recv, ring_send, ring_recv, mate_send, mate_recv,
     side_send, side_recv,
-    many_send, many_recv, back_send, back_recv,
+    many_send, many_recv, back_send, back_recv, row_sem,
 ):
     grp = lax.axis_index("grp")
     me = lax.axis_index("seq")
@@ -90,12 +131,11 @@
         )
 
     barrier = pltpu.get_barrier_semaphore()
-    near = (-2, -1, 1, 2)
-    for device in (
-        [(plane(step), me) for step in near]
-        + [(grp, to * 2 + core) for to in targets]
-        + [sibling]
-    ):
+    near = (-2, 2, -1, 1)
+    column = [(grp, (lax.rem(chip_y + n, SIDE) * SIDE + chip_x) * 2 + core) for n in (2, 1, 3)]
+    row = [(grp, (chip_y * SIDE + lax.rem(chip_x + n, SIDE)) * 2 + core) for n in (2, 1, 3)]
+    greeted = row + column + [(plane(step), me) for step in near] + [sibling]
+    for device in greeted:
         pl.semaphore_signal(barrier, inc=1, device_id=device, device_id_type=MESH)
 
     mine = pl.ds(pl.multiple_of(core * HALF, HALF), HALF)
@@ -206,17 +246,16 @@
     cot_copy = pltpu.make_async_copy(cot_in, cot4, local_sem.at[5])
     cot_copy.start()
 
-    pl.semaphore_wait(barrier, CHIPS + len(near))
+    pl.semaphore_wait(barrier, len(greeted))
+    for device in column:
+        pl.semaphore_signal(row_sem, inc=1, device_id=device, device_id_type=MESH)
     ring_start(0)
 
     for n in range(2):
         swaps[n].start()
 
-    lane = lax.broadcasted_iota(jnp.int32, (1, 128), 1)
-    low = jnp.where(lane < HEAD_DIM, 1.0, 0.0).astype(BF16)
-    high = jnp.where(lane < HEAD_DIM, 0.0, 1.0).astype(BF16)
-    low4 = jnp.concatenate([low] * 4, axis=1)
-    high4 = jnp.concatenate([high] * 4, axis=1)
+    low, high = head_masks(1)
+    low4, high4 = head_masks(4)
     row_id = lax.broadcasted_iota(jnp.int32, (128, 256), 0)
     col_id = lax.broadcasted_iota(jnp.int32, (128, 256), 1)
     bias[...] = jnp.where(lax.rem(row_id, 2) == lax.rem(col_id, 2), 0.0, -1e30)
@@ -282,6 +321,7 @@
         locals_[n].wait()
     for t in range(PAIRS):
         terms(wide(qh, t), wide(kh, t), s_send, t)
+    pl.semaphore_wait(row_sem, len(column))
     s_all = scatter(s_send, s_recv, 0)
     swaps[2].start()
     ring(2)
@@ -443,7 +483,7 @@
         dz = dz_rows[t]
         store(gvh, t, dot(gathered(p_all, 2 * t), dz * low4, TN)
               + dot(gathered(p_all, 2 * t + 1), dz * high4, TN))
-    returned = [give_back(gvh, gv_out, 0)]
+    local, away, landing = give_back(gvh, gv_out, 0)
 
     dz_rest.wait_send()
     g_rest.wait_recv()
@@ -454,23 +494,18 @@
     ds_rest = gather(ds_all, 5)
     out_copy.wait()
     g_rest.wait_send()
+    local.wait()
+    away.wait_send()
+    landing.wait_recv()
+    ds_rest.wait_send()
     ds_rest.wait_recv()
-    for t in range(PAIRS):
-        keys = wide(kh, t)
-        store(gqh, t, dot(gathered(ds_all, 2 * t), keys * low4, NN)
-              + dot(gathered(ds_all, 2 * t + 1), keys * high4, NN))
-    returned.append(give_back(gqh, gq_out, 1))
-    for t in range(PAIRS):
-        query = wide(qh, t)
-        store(gkh, t, dot(gathered(ds_all, 2 * t), query * low4, TN)
-              + dot(gathered(ds_all, 2 * t + 1), query * high4, TN))
-    returned.append(give_back(gkh, gk_out, 2))
-
-    ds_rest.wait_send()
-    for local, away, landing in returned:
-        local.wait()
-        away.wait_send()
-        landing.wait_recv()
+    ds_side = remote(ds_all, ds_out.at[core], back_send.at[1], back_recv.at[1], sibling)
+    ds_side.start()
+    ds_local = pltpu.make_async_copy(ds_all, ds_out.at[core], local_sem.at[8])
+    ds_local.start()
+    ds_local.wait()
+    ds_side.wait_send()
+    remote(ds_all, ds_out.at[other], back_send.at[1], back_recv.at[1], sibling).wait_recv()
 
 
 def on_device(planes, row_query, row_key, row_value, column_weight, cotangent):
@@ -480,12 +515,13 @@
     vmem = pltpu.VMEM
     sem = pltpu.SemaphoreType.DMA
     row_shape = jax.ShapeDtypeStruct((own_rows, columns, width), BF16)
-    shapes = (jax.ShapeDtypeStruct(cotangent.shape, BF16), row_shape, row_shape, row_shape)
-    results = pl.pallas_call(
+    out_shape = jax.ShapeDtypeStruct(cotangent.shape, BF16)
+    ds_shape = jax.ShapeDtypeStruct((2, CHIPS, 3, 16, 128), BF16)
+    column_output, grad_scores, grad_value = pl.pallas_call(
         functools.partial(kernel, planes),
-        out_shape=shapes,
+        out_shape=(out_shape, ds_shape, row_shape),
         in_specs=[pl.BlockSpec(memory_space=pl.ANY)] * 5,
-        out_specs=[pl.BlockSpec(memory_space=pl.ANY)] * 4,
+        out_specs=[pl.BlockSpec(memory_space=pl.ANY)] * 3,
         scratch_shapes=[
             vmem((4, 128, HALF), BF16),
             vmem((4, 128, HALF), BF16),
@@ -512,28 +548,30 @@
             vmem((CHIPS, 3, 16, 128), F32),
             vmem((CHIPS, 3, 16, 128), BF16),
             vmem((4, 128, HALF), BF16),
-            vmem((4, 128, HALF), BF16),
-            vmem((4, 128, HALF), BF16),
             sem((10,)),
             sem((3,)), sem((3,)),
             sem((2, planes)), sem((2, planes)),
             sem((2, planes)), sem((2, planes)),
             sem((2, planes, 2)), sem((2, planes, 2)),
             sem((6,)), sem((6,)),
-            sem((3,)), sem((3,)),
+            sem((2,)), sem((2,)),
+            pltpu.SemaphoreType.REGULAR,
         ],
         compiler_params=pltpu.CompilerParams(
             collective_id=0, has_side_effects=True, vmem_limit_bytes=VMEM_LIMIT
         ),
     )(row_query, row_key, row_value, column_weight.T, cotangent)
     return pl.pallas_call(
-        copy_out,
-        out_shape=shapes,
-        in_specs=[pl.BlockSpec(memory_space=pl.ANY)] * 4,
+        finish,
+        out_shape=(out_shape, row_shape, row_shape, row_shape),
+        in_specs=[pl.BlockSpec(memory_space=pl.ANY)] * 5,
         out_specs=[pl.BlockSpec(memory_space=pl.ANY)] * 4,
-        scratch_shapes=[vmem(x.shape, BF16) for x in shapes] + [sem((4 * PIECES,))] * 2,
+        scratch_shapes=[
+            vmem(x.shape, BF16)
+            for x in (row_shape, row_shape, ds_shape, out_shape, row_shape, row_shape, row_shape)
+        ] + [sem((5,)), sem((6,))],
         compiler_params=pltpu.CompilerParams(vmem_limit_bytes=VMEM_LIMIT),
-    )(*results)
+    )(row_query, row_key, grad_scores, column_output, grad_value)
 
 
 def solution(mesh):

time: 70.4 us -> 69.9 us (level)
  no operation moved by 1% of the time
where the time goes in v7:
time: 69.9 us; the launch traced here: 69.8 us
  Pallas kernels  69.2 us (99%)
    pallas_call x1, Pallas kernels, on_device(): pl.pallas_call(functools.partial(kernel, planes), out_shape=(out_shape, d...  66.5 us
    pallas_call x1, Pallas kernels, on_device(): pl.pallas_call(finish, out_shape=(out_shape, row_shape, row_shape, row_sh...  2.65 us

profile of v7, /device:TPU:1, one launch (start us, length us, event | category | flops | bytes accessed | tf_op | source)
XLA Modules:
  0.0 69.8 jit_solution(3763445549482008841)
XLA Ops:
  0.6 66.5 %shard_map.84 = (bf16[64,4,768]{2,1,0:T(4,128)(2,1)}, bf16[2,16,3,16,128]{4,3,2,1,0:T(8,128)(2,1)}, bf16[2,128,768]{2,1,0:T(8,128)(2,1)}) custom-call(bf16[2,128,768]{2,1,0:T(8,128)(2,1)} %q_in.3, bf16[2,128,768]{2,1,0:T(8,128)(2,1)} %k_in.3, bf16[2,128,768]{2,1,0:T(8,128)(2,1)} %v_in.1, bf16[144,768]{1,0:T(8,128)(2,1)} %bitcast.1, bf16[64,4,768]{2,1,0:T(4,128)(2,1)} %cot_in.1), custom_call_target="tpu_custom_call" | custom-call | tf_op jit(solution)/shard_map/pallas_call | solution.py:520
  67.1 2.6 %shard_map.85 = (bf16[64,4,768]{2,1,0:T(4,128)(2,1)}, bf16[2,128,768]{2,1,0:T(8,128)(2,1)}, bf16[2,128,768]{2,1,0:T(8,128)(2,1)}, bf16[2,128,768]{2,1,0:T(8,128)(2,1)}) custom-call(bf16[2,128,768]{2,1,0:T(8,128)(2,1)} %q_in.3, bf16[2,128,768]{2,1,0:T(8,128)(2,1)} %k_in.3, bf16[2,16,3,16,128]{4,3,2,1,0:T(8,128)(2,1)} %get-tuple-element.7.ds_in, ...), custom_call_target="tpu_custom_call" | custom-call | tf_op jit(solution)/shard_map/pallas_call | solution.py:564

commit v8 on v7

--- a/solution.py
+++ b/solution.py
@@ -415,9 +415,17 @@
             dabe[6 + u, rows[c]] = dot(dlogits[c], a2[c], NN).astype(BF16)
 
     dpacked = jnp.concatenate([dabe[n] for n in range(18)], axis=1)
+    pieces = [
+        dot(dpacked, weight[0, :, :256], NN),
+        dot(dpacked, jnp.concatenate([weight[0, :, 256:], weight[1, :, :128]], axis=1), NN),
+    ]
     for half in range(2):
         lanes = slice(half * HALF, half * HALF + HALF)
-        back = dot(dpacked, weight[half], NN)
+        if half == 0:
+            back = jnp.concatenate([pieces[0], pieces[1][:, :128]], axis=1)
+        else:
+            last = dot(dpacked, weight[1, :, 128:], NN)
+            back = jnp.concatenate([pieces[1][:, 128:], last], axis=1)
         blocks = jnp.concatenate(
             [
                 (cot[c, :, lanes].astype(F32) + back[128 * c : 128 * c + 128]).reshape(16, 8, HALF)

time: 69.9 us -> 70.9 us (1.014)
  Pallas kernels: 69.2 us -> 70.1 us
    pallas_call x1, Pallas kernels: 66.5 us -> 67.4 us  [on_device(): pl.pallas_call(functools.partial(kernel, planes), out_shape=(out_shape, d...]
where the time goes in v8:
time: 70.9 us; the launch traced here: 70.7 us
  Pallas kernels  70.1 us (99%)
    pallas_call x1, Pallas kernels, on_device(): pl.pallas_call(functools.partial(kernel, planes), out_shape=(out_shape, d...  67.4 us
    pallas_call x1, Pallas kernels, on_device(): pl.pallas_call(finish, out_shape=(out_shape, row_shape, row_shape, row_sh...  2.65 us

profile of v8, /device:TPU:1, one launch (start us, length us, event | category | flops | bytes accessed | tf_op | source)
XLA Modules:
  0.0 70.7 jit_solution(4424181474033999656)
XLA Ops:
  0.6 67.4 %shard_map.84 = (bf16[64,4,768]{2,1,0:T(4,128)(2,1)}, bf16[2,16,3,16,128]{4,3,2,1,0:T(8,128)(2,1)}, bf16[2,128,768]{2,1,0:T(8,128)(2,1)}) custom-call(bf16[2,128,768]{2,1,0:T(8,128)(2,1)} %q_in.3, bf16[2,128,768]{2,1,0:T(8,128)(2,1)} %k_in.3, bf16[2,128,768]{2,1,0:T(8,128)(2,1)} %v_in.1, bf16[144,768]{1,0:T(8,128)(2,1)} %bitcast.1, bf16[64,4,768]{2,1,0:T(4,128)(2,1)} %cot_in.1), custom_call_target="tpu_custom_call" | custom-call | tf_op jit(solution)/shard_map/pallas_call | solution.py:528
  68.1 2.6 %shard_map.85 = (bf16[64,4,768]{2,1,0:T(4,128)(2,1)}, bf16[2,128,768]{2,1,0:T(8,128)(2,1)}, bf16[2,128,768]{2,1,0:T(8,128)(2,1)}, bf16[2,128,768]{2,1,0:T(8,128)(2,1)}) custom-call(bf16[2,128,768]{2,1,0:T(8,128)(2,1)} %q_in.3, bf16[2,128,768]{2,1,0:T(8,128)(2,1)} %k_in.3, bf16[2,16,3,16,128]{4,3,2,1,0:T(8,128)(2,1)} %get-tuple-element.7.ds_in, ...), custom_call_target="tpu_custom_call" | custom-call | tf_op jit(solution)/shard_map/pallas_call | solution.py:572
